TPU v7x, 256 devices: a whole 4x4x8 slice. The times are simulated.
256 devices in a mesh: gx: 32 (over y_hi, z, core), gy: 8 (over y_lo, x).
Axes of the slice: x: 4, y: 4 (y_hi: 2, y_lo: 2; y = y_hi * 2 + y_lo), z: 8, core: 2. Of those that a mesh axis runs over, the one named last changes fastest.
Arguments:
- check_state: float32 [4, 288, 288, 192], P(None, 'gx', 'gy'), may hold values from -6 to 6
- syndrome: int32 [4, 288, 288], P(None, 'gx', 'gy'), may hold values 0 or 1
- left_state: float32 [4, 288, 288, 192], P(None, 'gx', 'gy'), may hold values from -6 to 6
- right_state: float32 [4, 288, 288, 192], P(None, 'gx', 'gy'), may hold values from -6 to 6
- offsets_one: int32 [6, 2], replicated, may hold values from -3 to 3, as said below
- offsets_two: int32 [6, 2], replicated, may hold values from -3 to 3, as said below
- syndrome_gain: float32 [192], replicated, may hold values from -6 to 6
- mix_one: float32 [6, 192, 192], replicated, may hold values from -0.4375 to 0.4375
- grow_one: float32 [2, 384, 384], replicated, may hold values from -0.3125 to 0.3125
- shrink_one: float32 [2, 384, 192], replicated, may hold values from -0.3125 to 0.3125
- mix_two: float32 [6, 192, 192], replicated, may hold values from -0.4375 to 0.4375
- grow_two: float32 [384, 384], replicated, may hold values from -0.3125 to 0.3125
- shrink_two: float32 [384, 192], replicated, may hold values from -0.3125 to 0.3125
Outputs:
- left_out: float32 [4, 288, 288, 192], P(None, 'gx', 'gy')
- right_out: float32 [4, 288, 288, 192], P(None, 'gx', 'gy')
- check_out: float32 [4, 288, 288, 192], P(None, 'gx', 'gy')
Inputs may be any that keep to these rules, and one draw needn't show every extreme that they name: `offsets_one`: each component of every offset lies between -3 and 3; in each layer and each of the two components, both ends are taken by some offset. `offsets_two`: each component of every offset lies between -3 and 3; in each layer and each of the two components, both ends are taken by some offset.
All inputs are finite; a program needn't handle non-finite values. No bound on the sum of `syndrome` on one device may be relied on, other than what follows from the above.
Results may differ from a plain program's by a relative error of at most 0.0001.
Values sent between devices are 32-bit elements; how exact they have to be, the bound alone decides.
No kernel may reach another device: no remote copies, remote signals or barrier semaphores. Data moves between devices by JAX's collectives and lax.ppermute only.
A program may use at most 128 MiB of HBM per device.

v0:
```python
import jax
import jax.numpy as jnp
from jax import lax
from jax.experimental import pallas as pl
from jax.experimental.pallas import tpu as pltpu
from jax.sharding import PartitionSpec as P

SPAN = 3
C = 192
F32 = jnp.float32
BF16 = jnp.bfloat16


def split(x):
    hi = x.astype(BF16)
    lo = (x - hi.astype(F32)).astype(BF16)
    return hi, lo


def packed(x):
    first, rest = x[:, :128], x[:, 128:]
    hi, lo = split(first)
    twice = jnp.concatenate([rest, rest], axis=1)
    rest_hi = twice.astype(BF16).astype(F32)
    lane = lax.broadcasted_iota(jnp.int32, twice.shape, 1)
    both = jnp.where(lane < 64, rest_hi, twice - rest_hi).astype(BF16)
    return [hi, both, lo]


def dot(a, b):
    return lax.dot_general(a, b, (((1,), (0,)), ((), ())), preferred_element_type=F32)


def dot_t(a, b):
    return lax.dot_general(a, b, (((1,), (1,)), ((), ())), preferred_element_type=F32)


def silu(v):
    return 0.5 * v * (1.0 + jnp.tanh(0.5 * v))


def vmem(count):
    return [pl.BlockSpec(memory_space=pltpu.VMEM)] * count


def params(mib):
    return pltpu.CompilerParams(vmem_limit_bytes=mib * 1024 * 1024)


HBM = pl.BlockSpec(memory_space=pltpu.HBM)


def far_off(*arrays):
    return [pltpu.with_memory_space_constraint(x, pltpu.HBM) for x in arrays]


def results(shapes, kind=F32):
    return [jax.ShapeDtypeStruct(shape, kind) for shape in shapes]


def fetch(pairs, sems):
    copies = [pltpu.make_async_copy(src, dst, sems.at[i]) for i, (src, dst) in enumerate(pairs)]
    for copy in copies:
        copy.start()
    return copies


def pair_rows(out, weights):
    hi, lo = split(weights)
    n = weights.shape[1]
    out[0:192, :n] = hi
    out[192:256, :n] = hi[128:192]
    out[256:384, :n] = hi[0:128]
    return lo


def low_rows(out, lo):
    n = lo.shape[1]
    out[0:192, :n] = lo
    out[192:256, :n] = jnp.zeros((64, n), BF16)


def picker():
    column = lax.broadcasted_iota(jnp.int32, (36, 8, 36), 0)
    lane = lax.broadcasted_iota(jnp.int32, (36, 8, 36), 2)
    return (column == lane).astype(F32)


def checks_row(check, syndrome, gain, pick):
    bits = (2 * syndrome - 1).astype(F32)
    bits = jnp.concatenate([bits, bits], axis=0)
    sign = jnp.sum(pick * bits[None], axis=-1, keepdims=True)[:, 0:4, :]
    return check + sign * gain


def is_odd():
    return lax.rem(lax.axis_index("gx"), 2)


def dense(value):
    half = value.shape[1] // 2
    rest = jnp.concatenate([value[:, :half, :, 128:], value[:, half:, :, 128:]], axis=-1)
    return jnp.concatenate([value[:, :, :, :128], rest], axis=1)


def undense(out, ref):
    columns = out.shape[1]
    half = columns // 2
    out[:, :, :, :128] = ref[:, :columns]
    out[:, :half, :, 128:] = ref[:, columns:, :, :64]
    out[:, half:, :, 128:] = ref[:, columns:, :, 64:]


def edges_kernel(check, syndrome, gain, near, far, first, last, rows, bits, gains, sems):
    copies = fetch(
        [(syndrome, bits), (gain, gains)] + [(check.at[r], rows.at[r]) for r in (0, 1, 2, 6, 7, 8)], sems
    )
    pick = picker()
    copies[0].wait()
    copies[1].wait()
    for n, r in enumerate((0, 1, 2, 6, 7, 8)):
        copies[2 + n].wait()
        value = checks_row(rows[r], bits[r], gains[...], pick)
        if r < 3:
            first[r] = value
        else:
            last[r - 6] = value
    odd = is_odd() == 1
    low, high = dense(first[...]), dense(last[...])
    near[...] = jnp.where(odd, low, high)
    far[...] = jnp.where(odd, high, low)


def make_edges(check, syndrome, gain):
    return pl.pallas_call(
        edges_kernel,
        out_shape=results([(3, 54, 4, 128)] * 2 + [(3, 36, 4, C)] * 2),
        in_specs=[HBM] * 3,
        out_specs=vmem(4),
        scratch_shapes=[
            pltpu.VMEM((9, 36, 4, C), F32), pltpu.VMEM((9, 4, 36), jnp.int32), pltpu.VMEM((1, C), F32),
            pltpu.SemaphoreType.DMA((8,)),
        ],
        name="edges",
        compiler_params=params(8),
    )(*far_off(check, syndrome, gain))


def prework_kernel(
    check, syndrome, gain, left, right, mix_one, grow_one, shrink_one, mix_two, grow_two, shrink_two,
    middle, m1, g1m, s1, m2, g2h, g2m, s2, left_q, right_q, left_g, right_g,
    g1h, rows, bits, gains, lefts, rights, mix_1, grow_1, shrink_1, mix_2, grow_2, shrink_2, sems,
):
    copies = fetch(
        [
            (left, lefts), (grow_one, grow_1), (right, rights), (mix_one, mix_1), (mix_two, mix_2),
            (shrink_one, shrink_1), (grow_two, grow_2), (shrink_two, shrink_2),
            (syndrome, bits), (gain, gains), (check.at[3:6], rows),
        ],
        sems,
    )

    def grow(src, out_h, out_m):
        for at, out in ((0, out_h), (192, out_m)):
            low_rows(out.at[384:640], pair_rows(out.at[0:384], src[at : at + 192, :]))

    def shrink(src, out):
        hi, lo = split(src[...])
        out[:, 0:384] = hi
        out[:, 384:768] = hi
        out[:, 768:1152] = lo

    for b, (ref, quart, half) in enumerate(((lefts, left_q, left_g), (rights, right_q, right_g))):
        copies[2 * b].wait()
        for q in range(4):
            quart[:, :, 4 * q : 4 * q + 4, :] = ref[:, 9 * q : 9 * q + 9]
        if b == 0:
            copies[1].wait()
        grow(grow_1.at[b], g1h, g1m.at[b])
        tiles = packed(quart[...].reshape(1296, C))
        half[...] = dot(jnp.concatenate(tiles + tiles[:2], axis=1), g1h[...]).reshape(9, 144, 384)
    copies[3].wait()
    copies[4].wait()
    copies[5].wait()
    for b in range(2):
        for k in range(3):
            low = pair_rows(m1.at[b, 384 * k : 384 * k + 384], mix_1[3 * b + k])
            low_rows(m1.at[b, 1152 + 256 * k : 1408 + 256 * k], low)
            out = m2.at[b, :, 256 * k : 256 * k + 256]
            low_rows(out.at[384:640], pair_rows(out.at[0:384], mix_2[3 * b + k]))
        shrink(shrink_1.at[b], s1.at[b])
    for copy in copies[6:]:
        copy.wait()
    grow(grow_2, g2h, g2m)
    shrink(shrink_2, s2)
    pick = picker()
    for r in range(3):
        middle[r] = checks_row(rows[r], bits[3 + r], gains[...], pick)


def prework(*operands):
    weights = [(2, 1920, C), (2, 640, 384), (2, C, 1152), (2, 640, 768), (640, 384), (640, 384), (C, 1152)]
    states = [(9, 9, 16, C)] * 2 + [(9, 144, 384)] * 2
    scratch = [(3, 36, 4, C), (9, 4, 36), (1, C), (9, 36, 4, C), (9, 36, 4, C), (6, C, C), (2, 384, 384)]
    scratch += [(2, C, 384), (6, C, C), (384, 384), (C, 384)]
    return pl.pallas_call(
        prework_kernel,
        out_shape=results([(3, 36, 4, C)]) + results(weights, BF16) + results(states),
        in_specs=[HBM] * 11,
        out_specs=vmem(12),
        scratch_shapes=[pltpu.VMEM((640, 384), BF16)]
        + [pltpu.VMEM(s, jnp.int32 if s == (9, 4, 36) else F32) for s in scratch]
        + [pltpu.SemaphoreType.DMA((11,))],
        name="prework",
        compiler_params=params(14),
    )(*far_off(*operands))


def columns_kernel(first, middle, last, near, far, low, high, top, bottom, rows):
    undense(rows.at[0], near)
    undense(rows.at[1], far)
    odd = is_odd()
    top[...] = rows[1 - odd]
    bottom[...] = rows[odd]
    for r, ref in enumerate((top, first, middle, last, bottom)):
        low[3 * r : 3 * r + 3] = ref[:, 0:3]
        high[3 * r : 3 * r + 3] = ref[:, 33:36]


def make_columns(*operands):
    return pl.pallas_call(
        columns_kernel,
        out_shape=results([(15, 3, 4, C)] * 2 + [(3, 36, 4, C)] * 2),
        in_specs=vmem(5),
        out_specs=vmem(4),
        scratch_shapes=[pltpu.VMEM((2, 3, 36, 4, C), F32)],
        name="columns",
        compiler_params=params(6),
    )(*operands)


def sums_kernel(acc_west, acc_east, near, far, low, high, top, bottom, rows):
    undense(rows.at[0], near)
    undense(rows.at[1], far)
    odd = is_odd()
    top[...] = rows[1 - odd]
    bottom[...] = rows[odd]
    for ref, acc, cols in ((low, acc_west, slice(0, 3)), (high, acc_east, slice(39, 42))):
        ref[0:3] = acc[0:3] + top[:, cols]
        ref[3:6] = acc[3:6]
        ref[6:9] = acc[6:9] + bottom[:, cols]


def make_sums(*operands):
    return pl.pallas_call(
        sums_kernel,
        out_shape=results([(9, 3, 4, C)] * 2 + [(3, 42, 4, C)] * 2),
        in_specs=vmem(4),
        out_specs=vmem(4),
        scratch_shapes=[pltpu.VMEM((2, 3, 42, 4, C), F32)],
        name="sums",
        compiler_params=params(6),
    )(*operands)


def fields_kernel(first, middle, last, top, bottom, g2h, pairs, west_q, east_q, checks_q, checks_g, field):
    for q in range(4):
        sub = slice(4 * q, 4 * q + 4)
        lo_j, hi_j = (3 if q == 0 else 0), (12 if q == 3 else 15)
        cols = slice(9 * q + lo_j - 3, 9 * q + hi_j - 3)
        for r, ref in enumerate((top, first, middle, last, bottom)):
            field[3 * r : 3 * r + 3, lo_j:hi_j, sub, :] = ref[:, cols]
    west_q[...] = field[:, 0:3]
    east_q[...] = field[:, 12:15]
    checks_q[...] = field[3:12, 3:12]
    tiles = packed(field[:, 3:12].reshape(2160, C))
    for t in range(3):
        pairs[:, :, :, 128 * t : 128 * t + 128] = tiles[t].reshape(15, 9, 16, 128)
    mid = pairs[3:12].reshape(1296, 384)
    checks_g[...] = dot(jnp.concatenate([mid, mid[:, :256]], axis=1), g2h[...])


def make_fields(first, middle, last, top, bottom, g2h):
    shapes = [(15, 3, 16, C), (15, 3, 16, C), (9, 9, 16, C), (1296, 384)]
    return pl.pallas_call(
        fields_kernel,
        out_shape=results([(15, 9, 16, 384)], BF16) + results(shapes),
        in_specs=vmem(6),
        out_specs=vmem(5),
        scratch_shapes=[pltpu.VMEM((15, 15, 16, C), F32)],
        name="fields",
        compiler_params=params(10),
    )(first, middle, last, top, bottom, g2h)


def update(h, half, m, grow, shrink):
    mean = jnp.sum(h * h + m * m, axis=-1, keepdims=True) * (1.0 / 384.0)
    mp = packed(m)
    inner = silu((dot(jnp.concatenate(mp + mp[:2], axis=1), grow[...]) + half) * lax.rsqrt(mean + 1e-05))
    hi, lo = split(inner)
    return h + dot_t(jnp.concatenate([hi, lo, hi], axis=1), shrink[...])


def block_step(b, starts, off_one, off_two, pairs, state, half, m1, g1m, s1, m2, acc, base):
    def windows(ref, *cols):
        parts = [ref[(pl.ds(at, 3), *cols)] for at in starts]
        return jnp.concatenate(parts, axis=0).reshape(432 * len(starts), ref.shape[-1])

    slabs = []
    for k in range(3):
        down, across = off_one[0, 3 * b + k], off_one[1, 3 * b + k]
        parts = [pairs[pl.ds(SPAN + at + down, 3), pl.ds(SPAN + across, 9)].reshape(432, 384) for at in starts]
        slabs.append(jnp.concatenate(parts, axis=0))
    m = dot(jnp.concatenate(slabs + [s[:, :256] for s in slabs], axis=1), m1[b])
    new = update(windows(state), windows(half), m, g1m.at[b], s1.at[b])
    tiles = packed(new)
    parts = dot(jnp.concatenate(tiles + tiles[:2], axis=1), m2[b])
    for k in range(3):
        down, across = off_two[0, 3 * b + k], off_two[1, 3 * b + k]
        for i, at in enumerate(starts):
            where = (pl.ds(base + at - down, 3), pl.ds(SPAN - across, 9))
            part = parts[432 * i : 432 * i + 432, 256 * k : 256 * k + 192]
            acc[where] = acc[where] + part.reshape(3, 9, 16, C)
    return new.reshape(3 * len(starts), 9, 16, C)


def to_sites(out, value):
    for q in range(4):
        out[:, 9 * q : 9 * q + 9] = value[:, :, 4 * q : 4 * q + 4, :]


def fold(acc, rows):
    for q in range(3):
        low, high = slice(4 * q, 4 * q + 4), slice(4 * q + 4, 4 * q + 8)
        acc[rows, 3:6, high, :] = acc[rows, 3:6, high, :] + acc[rows, 12:15, low, :]
        acc[rows, 9:12, low, :] = acc[rows, 9:12, low, :] + acc[rows, 0:3, high, :]


def outer_kernel(
    off_one, off_two, west, east, mid, west_q, east_q, left_q, right_q, left_g, right_g, m1, g1m, s1, m2,
    left_out, right_out, near, far, pairs, acc,
    side, fresh, whole, sems,
):
    pairs[:, 3:12] = mid[...]
    for at, known, new, sub in ((0, west_q, west, 0), (12, east_q, east, 12)):
        side[...] = known[...]
        side[:, :, sub : sub + 4, :] = new[...]
        tiles = packed(side[...].reshape(720, C))
        for t in range(3):
            pairs[:, at : at + 3, :, 128 * t : 128 * t + 128] = tiles[t].reshape(15, 3, 16, 128)
    acc[...] = jnp.zeros(acc.shape, F32)

    copies = []
    for b, (state, half, out) in enumerate(((left_q, left_g, left_out), (right_q, right_g, right_out))):
        new = block_step(b, (0, 6), off_one, off_two, pairs, state, half, m1, g1m, s1, m2, acc, SPAN)
        to_sites(fresh.at[b], new)
        for i, at in enumerate((0, 6)):
            copies.append(
                pltpu.make_async_copy(fresh.at[b, pl.ds(3 * i, 3)], out.at[pl.ds(at, 3)], sems.at[2 * b + i])
            )
            copies[-1].start()

    for n, at in enumerate((0, 12)):
        rows = slice(at, at + 3)
        fold(acc, rows)
        whole[n, :, 0:3] = acc[rows, 0:3, 0:4, :]
        to_sites(whole.at[n, :, 3:39], acc[rows, 3:12])
        whole[n, :, 39:42] = acc[rows, 12:15, 12:16, :]
    odd = is_odd()
    near[...] = dense(whole[1 - odd])
    far[...] = dense(whole[odd])
    for copy in copies:
        copy.wait()


def outer_rows(off_one, off_two, *operands):
    states = [jax.ShapeDtypeStruct((9, 36, 4, C), F32)] * 2
    smem = pl.BlockSpec(memory_space=pltpu.SMEM)
    return pl.pallas_call(
        outer_kernel,
        out_shape=states
        + results([(3, 63, 4, 128)] * 2)
        + results([(15, 15, 16, 384)], BF16)
        + results([(15, 15, 16, C)]),
        in_specs=[smem, smem] + vmem(13),
        out_specs=[HBM] * 2 + vmem(4),
        scratch_shapes=[
            pltpu.VMEM((15, 3, 16, C), F32),
            pltpu.VMEM((2, 6, 36, 4, C), F32),
            pltpu.VMEM((2, 3, 42, 4, C), F32),
            pltpu.SemaphoreType.DMA((4,)),
        ],
        name="outer_rows",
        compiler_params=params(18),
    )(off_one, off_two, *operands)


def inner_kernel(
    off_one, off_two, left_in, right_in, pairs, acc_in, left_q, right_q, left_g, right_g, m1, g1m, s1, m2,
    left_out, right_out, acc_mid, acc_west, acc_east,
    acc, fresh, sems,
):
    acc[...] = acc_in[3:12]
    copies = []
    for b, (state, half, out) in enumerate(((left_q, left_g, left_out), (right_q, right_g, right_out))):
        new = block_step(b, (3,), off_one, off_two, pairs, state, half, m1, g1m, s1, m2, acc, 0)
        to_sites(fresh.at[b], new)
        copies.append(pltpu.make_async_copy(fresh.at[b], out.at[pl.ds(3, 3)], sems.at[b]))
        copies[b].start()
    fold(acc, slice(0, 9))
    acc_mid[...] = acc[:, 3:12]
    acc_west[...] = acc[:, 0:3, 0:4, :]
    acc_east[...] = acc[:, 12:15, 12:16, :]
    for copy in copies:
        copy.wait()


def inner_rows(off_one, off_two, *operands):
    states = [jax.ShapeDtypeStruct((9, 36, 4, C), F32)] * 2
    smem = pl.BlockSpec(memory_space=pltpu.SMEM)
    return pl.pallas_call(
        inner_kernel,
        out_shape=states + results([(9, 9, 16, C), (9, 3, 4, C), (9, 3, 4, C)]),
        in_specs=[smem, smem, HBM, HBM] + vmem(10),
        out_specs=[HBM] * 2 + vmem(3),
        scratch_shapes=[
            pltpu.VMEM((9, 15, 16, C), F32),
            pltpu.VMEM((2, 3, 36, 4, C), F32),
            pltpu.SemaphoreType.DMA((2,)),
        ],
        input_output_aliases={2: 0, 3: 1},
        name="inner_rows",
        compiler_params=params(14),
    )(off_one, off_two, *operands)


def layer_two_kernel(
    from_top, from_bottom, from_west, from_east, acc_mid, checks_q, checks_g, g2m, s2, out, acc, fresh, sems
):
    acc[...] = acc_mid[...]
    for q in range(4):
        sub = slice(4 * q, 4 * q + 4)
        cols = slice(3 + 9 * q, 12 + 9 * q)
        acc[0:3, :, sub, :] = acc[0:3, :, sub, :] + from_top[:, cols]
        acc[6:9, :, sub, :] = acc[6:9, :, sub, :] + from_bottom[:, cols]
    acc[:, 0:3, 0:4, :] = acc[:, 0:3, 0:4, :] + from_west[...]
    acc[:, 6:9, 12:16, :] = acc[:, 6:9, 12:16, :] + from_east[...]
    new = update(checks_q[...].reshape(1296, C), checks_g[...], acc[...].reshape(1296, C), g2m, s2)
    whole = new.reshape(9, 9, 16, C)
    copies = []
    for g in range(3):
        rows = slice(3 * g, 3 * g + 3)
        to_sites(fresh.at[rows], whole[rows])
        copies.append(pltpu.make_async_copy(fresh.at[rows], out.at[rows], sems.at[g]))
        copies[g].start()
    for copy in copies:
        copy.wait()


def layer_two(from_top, from_bottom, from_west, from_east, *operands):
    return pl.pallas_call(
        layer_two_kernel,
        out_shape=jax.ShapeDtypeStruct((9, 36, 4, C), F32),
        in_specs=vmem(9),
        out_specs=HBM,
        scratch_shapes=[
            pltpu.VMEM((9, 9, 16, C), F32), pltpu.VMEM((9, 36, 4, C), F32), pltpu.SemaphoreType.DMA((3,)),
        ],
        name="layer_two",
        compiler_params=params(12),
    )(from_top, from_bottom, from_west, from_east, *operands)


def exchange(axis, low, high):
    count = lax.axis_size(axis)
    up = [(i, (i + 1) % count) for i in range(count)]
    return lax.ppermute(high, axis, up), lax.ppermute(low, axis, [(b, a) for a, b in up])


def trade(near, far):
    count = lax.axis_size("gx")
    next_chip = [(i, (i + (1 if i % 2 else -1)) % count) for i in range(count)]
    got = lax.ppermute(far, "gx", next_chip)
    return lax.ppermute(near, "gx", [(i, i ^ 1) for i in range(count)]), got


def body(
    check_state, syndrome, left_state, right_state, offsets_one, offsets_two, syndrome_gain,
    mix_one, grow_one, shrink_one, mix_two, grow_two, shrink_two,
):
    site = lambda x: jnp.transpose(x, (1, 2, 0, 3))
    back = lambda x: jnp.transpose(x, (2, 0, 1, 3))
    check, bits, gain = site(check_state), jnp.transpose(syndrome, (1, 0, 2)), syndrome_gain.reshape(1, C)
    near, far, first, last = make_edges(check, bits, gain)
    near, far = trade(near, far)
    middle, m1, g1m, s1, m2, g2h, g2m, s2, left_q, right_q, left_g, right_g = prework(
        check, bits, gain, site(left_state), site(right_state),
        mix_one, grow_one, jnp.swapaxes(shrink_one, 1, 2), mix_two, grow_two, shrink_two.T,
    )
    near, far, middle = lax.optimization_barrier((near, far, middle))
    low, high, top, bottom = make_columns(first, middle, last, near, far)
    west, east = exchange("gy", low, high)
    pairs, west_q, east_q, checks_q, checks_g = make_fields(first, middle, last, top, bottom, g2h)
    steps = (offsets_one.T, offsets_two.T)
    shared = (left_q, right_q, left_g, right_g, m1, g1m, s1, m2)
    left_out, right_out, near, far, pairs, acc = outer_rows(*steps, west, east, pairs, west_q, east_q, *shared)
    near, far = trade(near, far)
    left_out, right_out, acc_mid, acc_west, acc_east = inner_rows(*steps, left_out, right_out, pairs, acc, *shared)
    near, far, acc_mid = lax.optimization_barrier((near, far, acc_mid))
    low, high, from_top, from_bottom = make_sums(acc_west, acc_east, near, far)
    from_west, from_east = exchange("gy", low, high)
    check_out = layer_two(
        from_top, from_bottom, from_west, from_east, acc_mid, checks_q, checks_g, g2m, s2
    )
    return back(left_out), back(right_out), back(check_out)


def solution(mesh):
    site = P(None, "gx", "gy", None)
    in_specs = (site, P(None, "gx", "gy"), site, site) + (P(),) * 9
    return jax.shard_map(body, mesh=mesh, in_specs=in_specs, out_specs=(site,) * 3, check_vma=False)
```

profile of v0, /device:TPU:6, one launch (start us, length us, event | category | flops | bytes accessed | tf_op | source)
XLA Modules:
  0.0 61.9 jit_solution(8249987370366710602)
XLA Ops:
  0.6 1.9 %edges.1 = (f32[3,54,4,128]{3,2,1,0:T(4,128)S(1)}, f32[3,54,4,128]{3,2,1,0:T(4,128)S(1)}, f32[3,36,4,192]{3,2,1,0:T(4,128)S(1)}, f32[3,36,4,192]{3,2,1,0:T(4,128)S(1)}) custom-call(f32[9,36,4,192]{3,2,1,0:T(4,128)} %bitcast.16, s32[9,4,36]{2,1,0:T(4,128)} %bitcast.25, f32[1,192]{1,0:T(1,128)} %bitcast.27), custom_call_target="tpu_custom_call" | custom-call | tf_op jit(solution)/shard_map/edges/pallas_call | solution.py:135
  2.5 0.1 collective-permute-start
  2.6 8.6 %collective-permute-start.1 = (f32[3,54,4,128]{3,2,1,0:T(4,128)S(1)}, f32[3,54,4,128]{3,2,1,0:T(4,128)S(1)}, u32[]{:S(2)}, u32[]{:S(2)}) collective-permute-start(f32[3,54,4,128]{3,2,1,0:T(4,128)S(1)} %get-tuple-element.51), channel_id=1, source_target_pairs={{0,248},{8,16},{16,8},{24,32},{32,24},{40,48},{48,40},{56,64},{64,... | collective-permute-start | bytes 995336 | tf_op jit(solution)/shard_map/ppermute | solution.py:483
  11.2 5.5 %prework.1 = (f32[3,36,4,192]{3,2,1,0:T(4,128)S(1)}, bf16[2,1920,192]{2,1,0:T(8,128)(2,1)S(1)}, bf16[2,640,384]{2,1,0:T(8,128)(2,1)S(1)}, bf16[2,192,1152]{2,1,0...) custom-call(f32[9,36,4,192]{3,2,1,0:T(4,128)} %bitcast.17, ...), custom_call_target="tpu_custom_call" | custom-call | tf_op jit(solution)/shard_map/prework/pallas_call | solution.py:206
  16.7 0.0 collective-permute-done.near
  16.7 0.0 collective-permute-done.1.far
  16.8 0.3 columns.1
  17.1 0.7 %collective-permute-start.2 = (f32[15,3,4,192]{3,2,1,0:T(4,128)S(1)}, f32[15,3,4,192]{3,2,1,0:T(4,128)S(1)}, u32[]{:S(2)}, u32[]{:S(2)}) collective-permute-start(f32[15,3,4,192]{3,2,1,0:T(4,128)S(1)} %get-tuple-element.57), channel_id=1, source_target_pairs={{0,1},{1,2},{2,3},{3,4},{4,5},{5,6},{6,7},{7,0},{8,9},{9,10},{10,1... | collective-permute-start | bytes 414728 | tf_op jit(solution)/shard_map/ppermute | solution.py:477
  17.8 1.4 %collective-permute-start.3 = (f32[15,3,4,192]{3,2,1,0:T(4,128)S(1)}, f32[15,3,4,192]{3,2,1,0:T(4,128)S(1)}, u32[]{:S(2)}, u32[]{:S(2)}) collective-permute-start(f32[15,3,4,192]{3,2,1,0:T(4,128)S(1)} %get-tuple-element.58), channel_id=1, source_target_pairs={{1,0},{2,1},{3,2},{4,3},{5,4},{6,5},{7,6},{0,7},{9,8},{10,9},{11,1... | collective-permute-start | bytes 414728 | tf_op jit(solution)/shard_map/ppermute | solution.py:477
  19.2 1.9 %fields.1 = (bf16[15,9,16,384]{3,2,1,0:T(8,128)(2,1)S(1)}, f32[15,3,16,192]{3,2,1,0:T(8,128)S(1)}, f32[15,3,16,192]{3,2,1,0:T(8,128)S(1)}, f32[9,9,16,192]{3,2,1,0:T(8,128)S(1)}, f32[1296,384]{1,0:T(8,128)S(1)}) custom-call(f32[3,36,4,192]{3,2,1,0:T(4,128)S(1)} %get-tuple-element.49.first, f32[3,36,4,192]{3,2,1,0:T(4,128)S(1)} %get-tuple-element.53.middle, ...), custom_call_target="tpu_custom_call" | custom-call | tf_op jit(solution)/shard_map/fields/pallas_call | solution.py:285
  21.1 1.6 %collective-permute-done.2.west = f32[15,3,4,192]{3,2,1,0:T(4,128)S(1)} collective-permute-done((f32[15,3,4,192]{3,2,1,0:T(4,128)S(1)}, f32[15,3,4,192]{3,2,1,0:T(4,128)S(1)}, u32[]{:S(2)}, u32[]{:S(2)}) %collective-permute-start.2) | collective-permute-done | bytes 138272 | tf_op jit(solution)/shard_map/ppermute | solution.py:477
  22.7 2.7 %collective-permute-done.3.east = f32[15,3,4,192]{3,2,1,0:T(4,128)S(1)} collective-permute-done((f32[15,3,4,192]{3,2,1,0:T(4,128)S(1)}, f32[15,3,4,192]{3,2,1,0:T(4,128)S(1)}, u32[]{:S(2)}, u32[]{:S(2)}) %collective-permute-start.3) | collective-permute-done | bytes 138272 | tf_op jit(solution)/shard_map/ppermute | solution.py:477
  25.4 12.9 %outer_rows.1 = (f32[9,36,4,192]{3,2,1,0:T(4,128)}, f32[9,36,4,192]{3,2,1,0:T(4,128)}, f32[3,63,4,128]{3,2,1,0:T(4,128)S(1)}, f32[3,63,4,128]{3,2,1,0:T(4,128)S(...) custom-call(s32[2,6]{1,0:T(2,128)S(1)} %bitcast.12, s32[2,6]{1,0:T(2,128)S(1)} %bitcast.14, ...), custom_call_target="tpu_custom_call" | custom-call | tf_op jit(solution)/shard_map/outer_rows/pallas_call | solution.py:379
  38.4 0.1 collective-permute-start.4
  38.5 4.1 %collective-permute-start.5 = (f32[3,63,4,128]{3,2,1,0:T(4,128)S(1)}, f32[3,63,4,128]{3,2,1,0:T(4,128)S(1)}, u32[]{:S(2)}, u32[]{:S(2)}) collective-permute-start(f32[3,63,4,128]{3,2,1,0:T(4,128)S(1)} %get-tuple-element.82), channel_id=1, source_target_pairs={{0,248},{8,16},{16,8},{24,32},{32,24},{40,48},{48,40},{56,64},{64,... | collective-permute-start | bytes 1161224 | tf_op jit(solution)/shard_map/ppermute | solution.py:483
  42.6 7.3 %inner_rows.1 = (f32[9,36,4,192]{3,2,1,0:T(4,128)}, f32[9,36,4,192]{3,2,1,0:T(4,128)}, f32[9,9,16,192]{3,2,1,0:T(8,128)S(1)}, f32[9,3,4,192]{3,2,1,0:T(4,128)S(1)}, f32[9,3,4,192]{3,2,1,0:T(4,128)S(1)}) custom-call(s32[2,6]{1,0:T(2,128)S(1)} %bitcast.13, s32[2,6]{1,0:T(2,128)S(1)} %bitcast.15, ...), custom_call_target="tpu_custom_call", output_to_operand_aliasing={{0}: (2, {}), {1}: (3, {})} | custom-call | tf_op jit(solution)/shard_map/inner_rows/pallas_call | solution.py:421
  49.9 0.0 collective-permute-done.4.near
  49.9 0.0 collective-permute-done.5.far
  49.9 0.4 sums.1
  50.3 0.1 collective-permute-start.6
  50.4 2.0 %collective-permute-start.7 = (f32[9,3,4,192]{3,2,1,0:T(4,128)S(1)}, f32[9,3,4,192]{3,2,1,0:T(4,128)S(1)}, u32[]{:S(2)}, u32[]{:S(2)}) collective-permute-start(f32[9,3,4,192]{3,2,1,0:T(4,128)S(1)} %get-tuple-element.89), channel_id=1, source_target_pairs={{1,0},{2,1},{3,2},{4,3},{5,4},{6,5},{7,6},{0,7},{9,8},{10,9},{11,1... | collective-permute-start | bytes 248840 | tf_op jit(solution)/shard_map/ppermute | solution.py:477
  52.4 2.7 %collective-permute-done.6.from_west = f32[9,3,4,192]{3,2,1,0:T(4,128)S(1)} collective-permute-done((f32[9,3,4,192]{3,2,1,0:T(4,128)S(1)}, f32[9,3,4,192]{3,2,1,0:T(4,128)S(1)}, u32[]{:S(2)}, u32[]{:S(2)}) %collective-permute-start.6) | collective-permute-done | bytes 82976 | tf_op jit(solution)/shard_map/ppermute | solution.py:477
  55.1 2.2 %collective-permute-done.7.from_east = f32[9,3,4,192]{3,2,1,0:T(4,128)S(1)} collective-permute-done((f32[9,3,4,192]{3,2,1,0:T(4,128)S(1)}, f32[9,3,4,192]{3,2,1,0:T(4,128)S(1)}, u32[]{:S(2)}, u32[]{:S(2)}) %collective-permute-start.7) | collective-permute-done | bytes 82976 | tf_op jit(solution)/shard_map/ppermute | solution.py:477
  57.3 4.4 %layer_two.1 = f32[9,36,4,192]{3,2,1,0:T(4,128)} custom-call(f32[3,42,4,192]{3,2,1,0:T(4,128)S(1)} %get-tuple-element.86.from_top, f32[3,42,4,192]{3,2,1,0:T(4,128)S(1)} %get-tuple-element.87.from_bottom, f32[9,3,4,192]{3,2,1,0:T(4,128)S(1)} %collective-permute-done.6.from_west, f32[9,3,4,192]{3,2,1,0:T(4,128)S(1)} %collective-permute-done.7.from_east, ...), custom_call_target="tpu_custom_call" | custom-call | tf_op jit(solution)/shard_map/layer_two/pallas_call | solution.py:461
  (4 shorter events, 0.0 us)
Async XLA Ops:
  2.5 14.2 %collective-permute-start = (f32[3,54,4,128]{3,2,1,0:T(4,128)S(1)}, f32[3,54,4,128]{3,2,1,0:T(4,128)S(1)}, u32[]{:S(2)}, u32[]{:S(2)}) collective-permute-start(f32[3,54,4,128]{3,2,1,0:T(4,128)S(1)} %get-tuple-element.50), channel_id=1, source_target_pairs={{0,8},{8,0},{16,24},{24,16},{32,40},{40,32},{48,56},{56,48},{64,72... | collective-permute-start | bytes 995336 | tf_op jit(solution)/shard_map/ppermute | solution.py:484
  2.6 14.1 %collective-permute-start.1 = (f32[3,54,4,128]{3,2,1,0:T(4,128)S(1)}, f32[3,54,4,128]{3,2,1,0:T(4,128)S(1)}, u32[]{:S(2)}, u32[]{:S(2)}) collective-permute-start(f32[3,54,4,128]{3,2,1,0:T(4,128)S(1)} %get-tuple-element.51), channel_id=1, source_target_pairs={{0,248},{8,16},{16,8},{24,32},{32,24},{40,48},{48,40},{56,64},{64,... | collective-permute-start | bytes 995336 | tf_op jit(solution)/shard_map/ppermute | solution.py:483
  17.1 5.6 %collective-permute-start.2 = (f32[15,3,4,192]{3,2,1,0:T(4,128)S(1)}, f32[15,3,4,192]{3,2,1,0:T(4,128)S(1)}, u32[]{:S(2)}, u32[]{:S(2)}) collective-permute-start(f32[15,3,4,192]{3,2,1,0:T(4,128)S(1)} %get-tuple-element.57), channel_id=1, source_target_pairs={{0,1},{1,2},{2,3},{3,4},{4,5},{5,6},{6,7},{7,0},{8,9},{9,10},{10,1... | collective-permute-start | bytes 414728 | tf_op jit(solution)/shard_map/ppermute | solution.py:477
  17.8 7.6 %collective-permute-start.3 = (f32[15,3,4,192]{3,2,1,0:T(4,128)S(1)}, f32[15,3,4,192]{3,2,1,0:T(4,128)S(1)}, u32[]{:S(2)}, u32[]{:S(2)}) collective-permute-start(f32[15,3,4,192]{3,2,1,0:T(4,128)S(1)} %get-tuple-element.58), channel_id=1, source_target_pairs={{1,0},{2,1},{3,2},{4,3},{5,4},{6,5},{7,6},{0,7},{9,8},{10,9},{11,1... | collective-permute-start | bytes 414728 | tf_op jit(solution)/shard_map/ppermute | solution.py:477
  19.2 6.2 %copy-start = (s32[6,2]{0,1:T(2,128)S(1)}, s32[6,2]{0,1:T(2,128)}, u32[]{:S(2)}) copy-start(s32[6,2]{0,1:T(2,128)} %param.17) | copy-start | bytes 148
  19.2 6.2 %copy-start.1 = (s32[6,2]{0,1:T(2,128)S(1)}, s32[6,2]{0,1:T(2,128)}, u32[]{:S(2)}) copy-start(s32[6,2]{0,1:T(2,128)} %param.18) | copy-start | bytes 148
  38.4 11.5 %collective-permute-start.4 = (f32[3,63,4,128]{3,2,1,0:T(4,128)S(1)}, f32[3,63,4,128]{3,2,1,0:T(4,128)S(1)}, u32[]{:S(2)}, u32[]{:S(2)}) collective-permute-start(f32[3,63,4,128]{3,2,1,0:T(4,128)S(1)} %get-tuple-element.81), channel_id=1, source_target_pairs={{0,8},{8,0},{16,24},{24,16},{32,40},{40,32},{48,56},{56,48},{64,72... | collective-permute-start | bytes 1161224 | tf_op jit(solution)/shard_map/ppermute | solution.py:484
  38.5 11.4 %collective-permute-start.5 = (f32[3,63,4,128]{3,2,1,0:T(4,128)S(1)}, f32[3,63,4,128]{3,2,1,0:T(4,128)S(1)}, u32[]{:S(2)}, u32[]{:S(2)}) collective-permute-start(f32[3,63,4,128]{3,2,1,0:T(4,128)S(1)} %get-tuple-element.82), channel_id=1, source_target_pairs={{0,248},{8,16},{16,8},{24,32},{32,24},{40,48},{48,40},{56,64},{64,... | collective-permute-start | bytes 1161224 | tf_op jit(solution)/shard_map/ppermute | solution.py:483
  50.3 4.8 %collective-permute-start.6 = (f32[9,3,4,192]{3,2,1,0:T(4,128)S(1)}, f32[9,3,4,192]{3,2,1,0:T(4,128)S(1)}, u32[]{:S(2)}, u32[]{:S(2)}) collective-permute-start(f32[9,3,4,192]{3,2,1,0:T(4,128)S(1)} %get-tuple-element.88), channel_id=1, source_target_pairs={{0,1},{1,2},{2,3},{3,4},{4,5},{5,6},{6,7},{7,0},{8,9},{9,10},{10,1... | collective-permute-start | bytes 248840 | tf_op jit(solution)/shard_map/ppermute | solution.py:477
  50.4 6.9 %collective-permute-start.7 = (f32[9,3,4,192]{3,2,1,0:T(4,128)S(1)}, f32[9,3,4,192]{3,2,1,0:T(4,128)S(1)}, u32[]{:S(2)}, u32[]{:S(2)}) collective-permute-start(f32[9,3,4,192]{3,2,1,0:T(4,128)S(1)} %get-tuple-element.89), channel_id=1, source_target_pairs={{1,0},{2,1},{3,2},{4,3},{5,4},{6,5},{7,6},{0,7},{9,8},{10,9},{11,1... | collective-permute-start | bytes 248840 | tf_op jit(solution)/shard_map/ppermute | solution.py:477
where the time goes:
time: 62.1 us; the launch traced here: 61.9 us
  Pallas kernels  34.7 us (56%)
  starting transfers between devices  17.1 us (28%)
  waiting for transfers between devices  9.23 us (15%)
  between operations  0.93 us (1%)
    pallas_call x1, Pallas kernels, outer_rows(): pl.pallas_call(outer_kernel, out_shape=states + results([(3, 63, 4, 128)]...  12.9 us
    ppermute x2, starting transfers between devices, trade(): got = lax.ppermute(far, 'gx', next_chip)  12.7 us
    pallas_call x1, Pallas kernels, inner_rows(): pl.pallas_call(inner_kernel, out_shape=states + results([(9, 9, 16, C), (...  7.26 us
    pallas_call x1, Pallas kernels, prework(): pl.pallas_call(prework_kernel, out_shape=results([(3, 36, 4, C)]) + resul...  5.51 us
    ppermute x2, waiting for transfers between devices, exchange(): lax.ppermute(low, axis, [(b, a) for a, b in up])  4.91 us
    pallas_call x1, Pallas kernels, layer_two(): pl.pallas_call(layer_two_kernel, out_shape=jax.ShapeDtypeStruct((9, 36, 4...  4.44 us
    ppermute x2, waiting for transfers between devices, exchange(): lax.ppermute(high, axis, up)  4.31 us
    ppermute x2, starting transfers between devices, exchange(): lax.ppermute(low, axis, [(b, a) for a, b in up])  3.44 us
  transfers between devices with their start and end apart: 8, of which 4 were waited for; matrix products, arithmetic and copies ran while one was open for 0% of the time, Pallas kernels for 24%

commit v1 on v0

v1 whole, which is shorter than its diff:
```python
import jax
import jax.numpy as jnp
from jax import lax
from jax.experimental import pallas as pl
from jax.experimental.pallas import tpu as pltpu
from jax.sharding import PartitionSpec as P

SPAN = 3
C = 192
F32 = jnp.float32
BF16 = jnp.bfloat16


def split(x):
    hi = x.astype(BF16)
    lo = (x - hi.astype(F32)).astype(BF16)
    return hi, lo


def packed(x):
    first, rest = x[:, :128], x[:, 128:]
    hi, lo = split(first)
    twice = jnp.concatenate([rest, rest], axis=1)
    rest_hi = twice.astype(BF16).astype(F32)
    lane = lax.broadcasted_iota(jnp.int32, twice.shape, 1)
    both = jnp.where(lane < 64, rest_hi, twice - rest_hi).astype(BF16)
    return [hi, both, lo]


def dot(a, b):
    return lax.dot_general(a, b, (((1,), (0,)), ((), ())), preferred_element_type=F32)


def dot_t(a, b):
    return lax.dot_general(a, b, (((1,), (1,)), ((), ())), preferred_element_type=F32)


def silu(v):
    return 0.5 * v * (1.0 + jnp.tanh(0.5 * v))


def vmem(count):
    return [pl.BlockSpec(memory_space=pltpu.VMEM)] * count


def params(mib):
    return pltpu.CompilerParams(vmem_limit_bytes=mib * 1024 * 1024)


HBM = pl.BlockSpec(memory_space=pltpu.HBM)


def far_off(*arrays):
    return [pltpu.with_memory_space_constraint(x, pltpu.HBM) for x in arrays]


def results(shapes, kind=F32):
    return [jax.ShapeDtypeStruct(shape, kind) for shape in shapes]


def fetch(pairs, sems):
    copies = [pltpu.make_async_copy(src, dst, sems.at[i]) for i, (src, dst) in enumerate(pairs)]
    for copy in copies:
        copy.start()
    return copies


def pair_rows(out, weights):
    hi, lo = split(weights)
    n = weights.shape[1]
    out[0:192, :n] = hi
    out[192:256, :n] = hi[128:192]
    out[256:384, :n] = hi[0:128]
    return lo


def low_rows(out, lo):
    n = lo.shape[1]
    out[0:192, :n] = lo
    out[192:256, :n] = jnp.zeros((64, n), BF16)


def picker():
    column = lax.broadcasted_iota(jnp.int32, (36, 8, 36), 0)
    lane = lax.broadcasted_iota(jnp.int32, (36, 8, 36), 2)
    return (column == lane).astype(F32)


def checks_row(check, syndrome, gain, pick):
    bits = (2 * syndrome - 1).astype(F32)
    bits = jnp.concatenate([bits, bits], axis=0)
    sign = jnp.sum(pick * bits[None], axis=-1, keepdims=True)[:, 0:4, :]
    return check + sign * gain


def is_odd(axis="gx"):
    return lax.rem(lax.axis_index(axis), 2)


def dense(value):
    half = value.shape[1] // 2
    rest = jnp.concatenate([value[:, :half, :, 128:], value[:, half:, :, 128:]], axis=-1)
    return jnp.concatenate([value[:, :, :, :128], rest], axis=1)


def undense(out, ref):
    columns = out.shape[1]
    half = columns // 2
    out[:, :, :, :128] = ref[:, :columns]
    out[:, :half, :, 128:] = ref[:, columns:, :, :64]
    out[:, half:, :, 128:] = ref[:, columns:, :, 64:]


def edges_kernel(check, syndrome, gain, far, near, first, last, rows, bits, gains, sems):
    copies = fetch(
        [(syndrome, bits), (gain, gains)] + [(check.at[r], rows.at[r]) for r in (0, 1, 2, 6, 7, 8)], sems
    )
    pick = picker()
    copies[0].wait()
    copies[1].wait()
    for n, r in enumerate((0, 1, 2, 6, 7, 8)):
        copies[2 + n].wait()
        value = checks_row(rows[r], bits[r], gains[...], pick)
        if r < 3:
            first[r] = value
        else:
            last[r - 6] = value
    odd = is_odd() == 1
    low, high = dense(first[...]), dense(last[...])
    near[...] = jnp.where(odd, low, high)
    far[...] = jnp.where(odd, high, low)


def make_edges(check, syndrome, gain):
    return pl.pallas_call(
        edges_kernel,
        out_shape=results([(3, 54, 4, 128)] * 2 + [(3, 36, 4, C)] * 2),
        in_specs=[HBM] * 3,
        out_specs=vmem(4),
        scratch_shapes=[
            pltpu.VMEM((9, 36, 4, C), F32), pltpu.VMEM((9, 4, 36), jnp.int32), pltpu.VMEM((1, C), F32),
            pltpu.SemaphoreType.DMA((8,)),
        ],
        name="edges",
        compiler_params=params(8),
    )(*far_off(check, syndrome, gain))


def grow(src, out_h, out_m):
    for at, out in ((0, out_h), (192, out_m)):
        low_rows(out.at[384:640], pair_rows(out.at[0:384], src[at : at + 192, :]))


def shrink(src, out):
    hi, lo = split(src[...])
    out[:, 0:384] = hi
    out[:, 384:768] = hi
    out[:, 768:1152] = lo


def prework_kernel(
    check, syndrome, gain, left, right, mix_one, grow_one, shrink_one, mix_two, first, last,
    middle, m1, g1m, s1, m2, left_q, right_q, checks_q, left_g, right_g, center,
    g1h, rows, bits, gains, lefts, rights, mix_1, grow_1, shrink_1, mix_2, sems,
):
    copies = fetch(
        [
            (left, lefts), (grow_one, grow_1), (right, rights), (mix_one, mix_1), (mix_two, mix_2),
            (shrink_one, shrink_1), (syndrome, bits), (gain, gains), (check.at[3:6], rows),
        ],
        sems,
    )

    def mixes(b):
        for k in range(3):
            low = pair_rows(m1.at[b, 384 * k : 384 * k + 384], mix_1[3 * b + k])
            low_rows(m1.at[b, 1152 + 256 * k : 1408 + 256 * k], low)
            out = m2.at[b, :, 256 * k : 256 * k + 256]
            low_rows(out.at[384:640], pair_rows(out.at[0:384], mix_2[3 * b + k]))

    def half(b, ref, quart, out):
        copies[2 * b].wait()
        for q in range(4):
            quart[:, :, 4 * q : 4 * q + 4, :] = ref[:, 9 * q : 9 * q + 9]
        if b == 0:
            copies[1].wait()
        grow(grow_1.at[b], g1h.at[b], g1m.at[b])
        tiles = packed(quart[...].reshape(1296, C))
        yield
        out[...] = dot(jnp.concatenate(tiles + tiles[:2], axis=1), g1h[b]).reshape(9, 9, 16, 384)
        if b == 0:
            for copy in copies[3:6]:
                copy.wait()
        mixes(b)
        shrink(shrink_1.at[b], s1.at[b])
        yield

    def checks():
        yield
        for copy in copies[6:]:
            copy.wait()
        pick = picker()
        for r in range(3):
            middle[r] = checks_row(rows[r], bits[3 + r], gains[...], pick)
        for r, ref in enumerate((first, middle, last)):
            for q in range(4):
                checks_q[3 * r : 3 * r + 3, :, 4 * q : 4 * q + 4, :] = ref[:, 9 * q : 9 * q + 9]
        tiles = packed(checks_q[...].reshape(1296, C))
        for t in range(3):
            center[:, :, :, 128 * t : 128 * t + 128] = tiles[t].reshape(9, 9, 16, 128)

    together(half(0, lefts, left_q, left_g), half(1, rights, right_q, right_g), checks())


def prework(*operands):
    weights = [(2, 1920, C), (2, 640, 384), (2, C, 1152), (2, 640, 768)]
    states = [(9, 9, 16, C)] * 3 + [(9, 9, 16, 384)] * 2
    scratch = [(3, 36, 4, C), (9, 4, 36), (1, C), (9, 36, 4, C), (9, 36, 4, C), (6, C, C), (2, 384, 384)]
    scratch += [(2, C, 384), (6, C, C)]
    return pl.pallas_call(
        prework_kernel,
        out_shape=results([(3, 36, 4, C)])
        + results(weights, BF16)
        + results(states)
        + results([(9, 9, 16, 384)], BF16),
        in_specs=[HBM] * 9 + vmem(2),
        out_specs=vmem(11),
        scratch_shapes=[pltpu.VMEM((2, 640, 384), BF16)]
        + [pltpu.VMEM(s, jnp.int32 if s == (9, 4, 36) else F32) for s in scratch]
        + [pltpu.SemaphoreType.DMA((9,))],
        name="prework",
        compiler_params=params(18),
    )(*far_off(*operands[:9]), *operands[9:])


def columns_kernel(first, middle, last, near, far, to_far, to_near, top, bottom, rows, low, high):
    undense(rows.at[0], near)
    undense(rows.at[1], far)
    odd = is_odd()
    top[...] = rows[1 - odd]
    bottom[...] = rows[odd]
    for r, ref in enumerate((top, first, middle, last, bottom)):
        low[3 * r : 3 * r + 3] = ref[:, 0:3]
        high[3 * r : 3 * r + 3] = ref[:, 33:36]
    odd = is_odd("gy") == 1
    to_far[...] = jnp.where(odd, high[...], low[...])
    to_near[...] = jnp.where(odd, low[...], high[...])


def make_columns(*operands):
    return pl.pallas_call(
        columns_kernel,
        out_shape=results([(15, 3, 4, C)] * 2 + [(3, 36, 4, C)] * 2),
        in_specs=vmem(5),
        out_specs=vmem(4),
        scratch_shapes=[pltpu.VMEM((2, 3, 36, 4, C), F32)] + [pltpu.VMEM((15, 3, 4, C), F32)] * 2,
        name="columns",
        compiler_params=params(6),
    )(*operands)


def sums_kernel(acc_west, acc_east, near, far, to_far, to_near, top, bottom, rows, low, high):
    undense(rows.at[0], near)
    undense(rows.at[1], far)
    odd = is_odd()
    top[...] = rows[1 - odd]
    bottom[...] = rows[odd]
    for ref, acc, cols in ((low, acc_west, slice(0, 3)), (high, acc_east, slice(39, 42))):
        ref[0:3] = acc[0:3] + top[:, cols]
        ref[3:6] = acc[3:6]
        ref[6:9] = acc[6:9] + bottom[:, cols]
    odd = is_odd("gy") == 1
    to_far[...] = jnp.where(odd, high[...], low[...])
    to_near[...] = jnp.where(odd, low[...], high[...])


def make_sums(*operands):
    return pl.pallas_call(
        sums_kernel,
        out_shape=results([(9, 3, 4, C)] * 2 + [(3, 42, 4, C)] * 2),
        in_specs=vmem(4),
        out_specs=vmem(4),
        scratch_shapes=[pltpu.VMEM((2, 3, 42, 4, C), F32)] + [pltpu.VMEM((9, 3, 4, C), F32)] * 2,
        name="sums",
        compiler_params=params(6),
    )(*operands)


def update(h, half, m, grow, shrink):
    mean = jnp.sum(h * h + m * m, axis=-1, keepdims=True) * (1.0 / 384.0)
    mp = packed(m)
    yield
    grown = dot(jnp.concatenate(mp + mp[:2], axis=1), grow[...])
    yield
    hi, lo = split(silu((grown + half) * lax.rsqrt(mean + 1e-05)))
    yield
    yield h + dot_t(jnp.concatenate([hi, lo, hi], axis=1), shrink[...])


def together(*steps):
    last = [None] * len(steps)
    live = list(range(len(steps)))
    while live:
        for i in list(live):
            try:
                last[i] = next(steps[i])
            except StopIteration:
                live.remove(i)
    return last


def block_step(b, pieces, off_one, off_two, pairs, margin, state, half, m1, g1m, s1, m2, acc, base):
    sizes = [48 * wide for _, _, wide in pieces]

    def windows(ref, down=0, across=0):
        parts = [
            ref[pl.ds(row + down, 3), pl.ds(col + across, wide)].reshape(48 * wide, ref.shape[-1])
            for row, col, wide in pieces
        ]
        return jnp.concatenate(parts, axis=0)

    slabs = [
        windows(pairs, SPAN + off_one[0, 3 * b + k], margin + off_one[1, 3 * b + k]) for k in range(3)
    ]
    m = dot(jnp.concatenate(slabs + [s[:, :256] for s in slabs], axis=1), m1[b])
    yield
    for new in update(windows(state), windows(half), m, g1m.at[b], s1.at[b]):
        yield
    tiles = packed(new)
    yield
    parts = dot(jnp.concatenate(tiles + tiles[:2], axis=1), m2[b])
    yield
    for k in range(3):
        down, across = off_two[0, 3 * b + k], off_two[1, 3 * b + k]
        at = 0
        for size, (row, col, wide) in zip(sizes, pieces):
            where = (pl.ds(base + row - down, 3), pl.ds(SPAN + col - across, wide))
            acc[where] = acc[where] + parts[at : at + size, 256 * k : 256 * k + 192].reshape(3, wide, 16, C)
            at += size
    at, news = 0, []
    for size, (row, col, wide) in zip(sizes, pieces):
        news.append(new[at : at + size].reshape(3, wide, 16, C))
        at += size
    yield news


def layer_one_steps(pieces, off_one, off_two, pairs, margin, states, halves, m1, g1m, s1, m2, acc, base):
    return together(
        *(
            block_step(b, pieces, off_one, off_two, pairs, margin, states[b], halves[b], m1, g1m, s1, m2, acc, base)
            for b in range(2)
        )
    )


def to_sites(out, value, col=0):
    for q in range(4):
        out[:, 9 * q + col : 9 * q + col + value.shape[1]] = value[:, :, 4 * q : 4 * q + 4, :]


def fold(acc, rows):
    for q in range(3):
        low, high = slice(4 * q, 4 * q + 4), slice(4 * q + 4, 4 * q + 8)
        acc[rows, 3:6, high, :] = acc[rows, 3:6, high, :] + acc[rows, 12:15, low, :]
        acc[rows, 9:12, low, :] = acc[rows, 9:12, low, :] + acc[rows, 0:3, high, :]


def core_kernel(
    off_one, off_two, first, middle, last, top, bottom, center, left_q, right_q, left_g, right_g, m1, g1m, s1, m2,
    mid, west_q, east_q, acc, left_core, right_core,
    field,
):
    mid[3:12] = center[...]
    for at, ref in ((0, top), (12, bottom)):
        for q in range(4):
            field[:, :, 4 * q : 4 * q + 4, :] = ref[:, 9 * q : 9 * q + 9]
        tiles = packed(field[...].reshape(432, C))
        for t in range(3):
            mid[at : at + 3, :, :, 128 * t : 128 * t + 128] = tiles[t].reshape(3, 9, 16, 128)
    for r, ref in enumerate((top, first, middle, last, bottom)):
        for q in range(3):
            east_q[3 * r : 3 * r + 3, :, 4 * q : 4 * q + 4, :] = ref[:, 9 * q + 9 : 9 * q + 12]
            west_q[3 * r : 3 * r + 3, :, 4 * q + 4 : 4 * q + 8, :] = ref[:, 9 * q + 6 : 9 * q + 9]
    acc[...] = jnp.zeros(acc.shape, F32)
    news = layer_one_steps(
        [(0, 3, 3), (6, 3, 3)], off_one, off_two, mid, 0, (left_q, right_q), (left_g, right_g), m1, g1m, s1, m2, acc,
        SPAN,
    )
    for ref, (low, high) in zip((left_core, right_core), news):
        ref[0:3] = low
        ref[3:6] = high


def core_columns(off_one, off_two, *operands):
    smem = pl.BlockSpec(memory_space=pltpu.SMEM)
    shapes = [(15, 3, 16, C), (15, 3, 16, C), (15, 15, 16, C), (6, 3, 16, C), (6, 3, 16, C)]
    return pl.pallas_call(
        core_kernel,
        out_shape=results([(15, 9, 16, 384)], BF16) + results(shapes),
        in_specs=[smem, smem] + vmem(14),
        out_specs=vmem(6),
        scratch_shapes=[pltpu.VMEM((3, 9, 16, C), F32)],
        name="core_columns",
        compiler_params=params(12),
    )(off_one, off_two, *operands)


def outer_kernel(
    off_one, off_two, near_in, far_in, mid, west_q, east_q, acc_core, left_core, right_core,
    left_q, right_q, left_g, right_g, m1, g1m, s1, m2,
    left_out, right_out, far, near, pairs, acc,
    side, fresh, whole, sems,
):
    pairs[:, 3:12] = mid[...]
    odd = is_odd("gy") == 1
    west = jnp.where(odd, near_in[...], far_in[...])
    east = jnp.where(odd, far_in[...], near_in[...])
    for at, known, new, sub in ((0, west_q, west, 0), (12, east_q, east, 12)):
        side[...] = known[...]
        side[:, :, sub : sub + 4, :] = new
        tiles = packed(side[...].reshape(720, C))
        for t in range(3):
            pairs[:, at : at + 3, :, 128 * t : 128 * t + 128] = tiles[t].reshape(15, 3, 16, 128)
    acc[...] = acc_core[...]
    pieces = [(0, 0, 3), (0, 6, 3), (6, 0, 3), (6, 6, 3)]
    news = layer_one_steps(
        pieces, off_one, off_two, pairs, SPAN, (left_q, right_q), (left_g, right_g), m1, g1m, s1, m2, acc, SPAN
    )
    copies = []
    for b, (new, core, out) in enumerate(zip(news, (left_core, right_core), (left_out, right_out))):
        to_sites(fresh.at[b], core[...], 3)
        for (row, col, _), value in zip(pieces, new):
            to_sites(fresh.at[b, row // 2 : row // 2 + 3], value, col)
        for i, at in enumerate((0, 6)):
            copies.append(
                pltpu.make_async_copy(fresh.at[b, pl.ds(3 * i, 3)], out.at[pl.ds(at, 3)], sems.at[2 * b + i])
            )
            copies[-1].start()

    for n, at in enumerate((0, 12)):
        rows = slice(at, at + 3)
        fold(acc, rows)
        whole[n, :, 0:3] = acc[rows, 0:3, 0:4, :]
        to_sites(whole.at[n, :, 3:39], acc[rows, 3:12])
        whole[n, :, 39:42] = acc[rows, 12:15, 12:16, :]
    odd = is_odd()
    near[...] = dense(whole[1 - odd])
    far[...] = dense(whole[odd])
    for copy in copies:
        copy.wait()


def outer_rows(off_one, off_two, *operands):
    states = [jax.ShapeDtypeStruct((9, 36, 4, C), F32)] * 2
    smem = pl.BlockSpec(memory_space=pltpu.SMEM)
    return pl.pallas_call(
        outer_kernel,
        out_shape=states
        + results([(3, 63, 4, 128)] * 2)
        + results([(15, 15, 16, 384)], BF16)
        + results([(15, 15, 16, C)]),
        in_specs=[smem, smem] + vmem(16),
        out_specs=[HBM] * 2 + vmem(4),
        scratch_shapes=[
            pltpu.VMEM((15, 3, 16, C), F32),
            pltpu.VMEM((2, 6, 36, 4, C), F32),
            pltpu.VMEM((2, 3, 42, 4, C), F32),
            pltpu.SemaphoreType.DMA((4,)),
        ],
        name="outer_rows",
        compiler_params=params(18),
    )(off_one, off_two, *operands)


def inner_kernel(
    off_one, off_two, left_in, right_in, grow_two, shrink_two, pairs, acc_in, center,
    left_q, right_q, left_g, right_g, m1, g1m, s1, m2,
    left_out, right_out, acc_mid, acc_west, acc_east, checks_g, g2m, s2,
    acc, fresh, grow_2, shrink_2, g2h, sems,
):
    loads = [
        pltpu.make_async_copy(src, dst, sems.at[2 + i])
        for i, (src, dst) in enumerate(((grow_two, grow_2), (shrink_two, shrink_2)))
    ]
    for copy in loads:
        copy.start()
    acc[...] = acc_in[3:12]
    copies = []
    news = layer_one_steps(
        [(3, 0, 9)], off_one, off_two, pairs, SPAN, (left_q, right_q), (left_g, right_g), m1, g1m, s1, m2, acc, 0
    )
    for b, ((new,), out) in enumerate(zip(news, (left_out, right_out))):
        to_sites(fresh.at[b], new)
        copies.append(pltpu.make_async_copy(fresh.at[b], out.at[pl.ds(3, 3)], sems.at[b]))
        copies[b].start()
    for copy in loads:
        copy.wait()
    grow(grow_2, g2h, g2m)
    shrink(shrink_2, s2)
    tiles = center[...].reshape(1296, 384)
    checks_g[...] = dot(jnp.concatenate([tiles, tiles[:, :256]], axis=1), g2h[...]).reshape(9, 9, 16, 384)
    fold(acc, slice(0, 9))
    acc_mid[...] = acc[:, 3:12]
    acc_west[...] = acc[:, 0:3, 0:4, :]
    acc_east[...] = acc[:, 12:15, 12:16, :]
    for copy in copies:
        copy.wait()


def inner_rows(off_one, off_two, left_out, right_out, grow_two, shrink_two, *operands):
    states = [jax.ShapeDtypeStruct((9, 36, 4, C), F32)] * 2
    smem = pl.BlockSpec(memory_space=pltpu.SMEM)
    return pl.pallas_call(
        inner_kernel,
        out_shape=states
        + results([(9, 9, 16, C), (9, 3, 4, C), (9, 3, 4, C), (9, 9, 16, 384)])
        + results([(640, 384), (C, 1152)], BF16),
        in_specs=[smem, smem] + [HBM] * 4 + vmem(11),
        out_specs=[HBM] * 2 + vmem(6),
        scratch_shapes=[
            pltpu.VMEM((9, 15, 16, C), F32),
            pltpu.VMEM((2, 3, 36, 4, C), F32),
            pltpu.VMEM((384, 384), F32),
            pltpu.VMEM((C, 384), F32),
            pltpu.VMEM((640, 384), BF16),
            pltpu.SemaphoreType.DMA((4,)),
        ],
        input_output_aliases={2: 0, 3: 1},
        name="inner_rows",
        compiler_params=params(16),
    )(off_one, off_two, left_out, right_out, *far_off(grow_two, shrink_two), *operands)


def all_columns_kernel(
    from_top, from_bottom, acc_mid, checks_q, checks_g, g2m, s2, out, edge_m, edge_h, edge_g, acc, fresh, sems
):
    acc[...] = acc_mid[...]
    for q in range(4):
        sub = slice(4 * q, 4 * q + 4)
        cols = slice(3 + 9 * q, 12 + 9 * q)
        acc[0:3, :, sub, :] = acc[0:3, :, sub, :] + from_top[:, cols]
        acc[6:9, :, sub, :] = acc[6:9, :, sub, :] + from_bottom[:, cols]
    for edge, whole in ((edge_m, acc), (edge_h, checks_q), (edge_g, checks_g)):
        edge[:, :, 0:4, :] = whole[:, 0:3, 0:4, :]
        edge[:, :, 4:8, :] = whole[:, 6:9, 12:16, :]
    groups = (slice(0, 5), slice(5, 9))
    news = together(
        *(
            update(checks_q[r].reshape(-1, C), checks_g[r].reshape(-1, 384), acc[r].reshape(-1, C), g2m, s2)
            for r in groups
        )
    )
    copies = []
    for g, (rows, new) in enumerate(zip(groups, news)):
        to_sites(fresh.at[rows], new.reshape(-1, 9, 16, C))
        copies.append(pltpu.make_async_copy(fresh.at[rows], out.at[rows], sems.at[g]))
        copies[g].start()
    for copy in copies:
        copy.wait()


def all_columns(*operands):
    return pl.pallas_call(
        all_columns_kernel,
        out_shape=[jax.ShapeDtypeStruct((9, 36, 4, C), F32)]
        + results([(9, 3, 8, C), (9, 3, 8, C), (9, 3, 8, 384)]),
        in_specs=vmem(7),
        out_specs=[HBM] + vmem(3),
        scratch_shapes=[
            pltpu.VMEM((9, 9, 16, C), F32), pltpu.VMEM((9, 36, 4, C), F32), pltpu.SemaphoreType.DMA((2,)),
        ],
        name="all_columns",
        compiler_params=params(14),
    )(*operands)


def edge_columns_kernel(out_in, near, far, edge_m, edge_h, edge_g, g2m, s2, out, message, fresh, sems):
    message[...] = edge_m[...]
    odd = is_odd("gy") == 1
    message[:, :, 0:4, :] = message[:, :, 0:4, :] + jnp.where(odd, near[...], far[...])
    message[:, :, 4:8, :] = message[:, :, 4:8, :] + jnp.where(odd, far[...], near[...])
    (new,) = together(
        update(edge_h[...].reshape(216, C), edge_g[...].reshape(216, 384), message[...].reshape(216, C), g2m, s2)
    )
    new = new.reshape(9, 3, 8, C)
    copies = []
    for n, at in enumerate((0, 33)):
        fresh[n] = new[:, :, 4 * n : 4 * n + 4, :]
        copies.append(pltpu.make_async_copy(fresh.at[n], out.at[:, pl.ds(at, 3)], sems.at[n]))
        copies[n].start()
    for copy in copies:
        copy.wait()


def edge_columns(*operands):
    return pl.pallas_call(
        edge_columns_kernel,
        out_shape=jax.ShapeDtypeStruct((9, 36, 4, C), F32),
        in_specs=[HBM] + vmem(7),
        out_specs=HBM,
        scratch_shapes=[
            pltpu.VMEM((9, 3, 8, C), F32), pltpu.VMEM((2, 9, 3, 4, C), F32), pltpu.SemaphoreType.DMA((2,)),
        ],
        input_output_aliases={0: 0},
        name="edge_columns",
        compiler_params=params(8),
    )(*operands)


def trade(near, far, axis):
    count = lax.axis_size(axis)
    beyond = [(i, (i + (1 if i % 2 else -1)) % count) for i in range(count)]
    got = lax.ppermute(far, axis, beyond)
    return lax.ppermute(near, axis, [(i, i ^ 1) for i in range(count)]), got


def body(
    check_state, syndrome, left_state, right_state, offsets_one, offsets_two, syndrome_gain,
    mix_one, grow_one, shrink_one, mix_two, grow_two, shrink_two,
):
    site = lambda x: jnp.transpose(x, (1, 2, 0, 3))
    back = lambda x: jnp.transpose(x, (2, 0, 1, 3))
    check, bits, gain = site(check_state), jnp.transpose(syndrome, (1, 0, 2)), syndrome_gain.reshape(1, C)
    far, near, first, last = make_edges(check, bits, gain)
    near, far = trade(near, far, "gx")
    middle, m1, g1m, s1, m2, left_q, right_q, checks_q, left_g, right_g, center = prework(
        check, bits, gain, site(left_state), site(right_state),
        mix_one, grow_one, jnp.swapaxes(shrink_one, 1, 2), mix_two, first, last,
    )
    near, far, middle = lax.optimization_barrier((near, far, middle))
    far, near, top, bottom = make_columns(first, middle, last, near, far)
    near, far = trade(near, far, "gy")
    steps = (offsets_one.T, offsets_two.T)
    shared = (left_q, right_q, left_g, right_g, m1, g1m, s1, m2)
    core = core_columns(*steps, first, middle, last, top, bottom, center, *shared)
    left_out, right_out, far, near, pairs, acc = outer_rows(*steps, near, far, *core, *shared)
    near, far = trade(near, far, "gx")
    left_out, right_out, acc_mid, acc_west, acc_east, checks_g, g2m, s2 = inner_rows(
        *steps, left_out, right_out, grow_two, shrink_two.T, pairs, acc, center, *shared
    )
    near, far, acc_mid = lax.optimization_barrier((near, far, acc_mid))
    far, near, from_top, from_bottom = make_sums(acc_west, acc_east, near, far)
    near, far = trade(near, far, "gy")
    check_out, edge_m, edge_h, edge_g = all_columns(from_top, from_bottom, acc_mid, checks_q, checks_g, g2m, s2)
    check_out = edge_columns(check_out, near, far, edge_m, edge_h, edge_g, g2m, s2)
    return back(left_out), back(right_out), back(check_out)


def solution(mesh):
    site = P(None, "gx", "gy", None)
    in_specs = (site, P(None, "gx", "gy"), site, site) + (P(),) * 9
    return jax.shard_map(body, mesh=mesh, in_specs=in_specs, out_specs=(site,) * 3, check_vma=False)
```

time: 62.1 us -> 54 us (0.87)
  Pallas kernels: 34.7 us -> 31.5 us
  waiting for transfers between devices: 9.23 us -> 6.29 us
  starting transfers between devices: 17.1 us -> 15.2 us
    pallas_call x1, Pallas kernels: 12.9 us -> 7.12 us  [outer_rows(): pl.pallas_call(outer_kernel, out_shape=states + results([(3, 63, 4, 128)]...]
    pallas_call x2 -> x3, Pallas kernels: 6.35 us -> 9.32 us  [the longest x1 4.07 us: core_columns(): pl.pallas_call(core_kernel, out_shape=results([(15, 9, 16, 384)], BF16) +...]
    ppermute x8, waiting for transfers between devices: 9.23 us -> 6.29 us  [the longest x4 6.28 us: trade(): got = lax.ppermute(far, axis, beyond)]
    ppermute x8, starting transfers between devices: 17.1 us -> 15.2 us  [the longest x4 14 us: trade(): got = lax.ppermute(far, axis, beyond)]
    pallas_call x1, Pallas kernels: 7.26 us -> 6.14 us  [inner_rows(): pl.pallas_call(inner_kernel, out_shape=states + results([(9, 9, 16, C), (...]
    pallas_call x1, Pallas kernels: 5.51 us -> 6.18 us  [prework(): pl.pallas_call(prework_kernel, out_shape=results([(3, 36, 4, C)]) + resul...]
  transfers between devices with their start and end apart: 8 -> 8, of which waited for: 4 -> 3; matrix products, arithmetic and copies ran while one was open for 0% -> 0% of each run, Pallas kernels for 24% -> 37%
where the time goes in v1:
time: 54 us; the launch traced here: 53.9 us
  Pallas kernels  31.5 us (58%)
  starting transfers between devices  15.2 us (28%)
  waiting for transfers between devices  6.29 us (12%)
  between operations  0.96 us (2%)
    ppermute x4, starting transfers between devices, trade(): got = lax.ppermute(far, axis, beyond)  14 us
    pallas_call x1, Pallas kernels, outer_rows(): pl.pallas_call(outer_kernel, out_shape=states + results([(3, 63, 4, 128)]...  7.12 us
    ppermute x4, waiting for transfers between devices, trade(): got = lax.ppermute(far, axis, beyond)  6.28 us
    pallas_call x1, Pallas kernels, prework(): pl.pallas_call(prework_kernel, out_shape=results([(3, 36, 4, C)]) + resul...  6.18 us
    pallas_call x1, Pallas kernels, inner_rows(): pl.pallas_call(inner_kernel, out_shape=states + results([(9, 9, 16, C), (...  6.14 us
    pallas_call x1, Pallas kernels, core_columns(): pl.pallas_call(core_kernel, out_shape=results([(15, 9, 16, 384)], BF16) +...  4.07 us
    pallas_call x1, Pallas kernels, all_columns(): pl.pallas_call(all_columns_kernel, out_shape=[jax.ShapeDtypeStruct((9, 36...  3.68 us
    pallas_call x1, Pallas kernels, make_edges(): pl.pallas_call(edges_kernel, out_shape=results([(3, 54, 4, 128)] * 2 + [(...  1.89 us
  transfers between devices with their start and end apart: 8, of which 3 were waited for; matrix products, arithmetic and copies ran while one was open for 0% of the time, Pallas kernels for 37%

profile of v1, /device:TPU:6, one launch (start us, length us, event | category | flops | bytes accessed | tf_op | source)
XLA Modules:
  0.0 53.9 jit_solution(143669465672719887)
XLA Ops:
  0.6 1.9 %edges.1 = (f32[3,54,4,128]{3,2,1,0:T(4,128)S(1)}, f32[3,54,4,128]{3,2,1,0:T(4,128)S(1)}, f32[3,36,4,192]{3,2,1,0:T(4,128)S(1)}, f32[3,36,4,192]{3,2,1,0:T(4,128)S(1)}) custom-call(f32[9,36,4,192]{3,2,1,0:T(4,128)} %bitcast.18, s32[9,4,36]{2,1,0:T(4,128)} %bitcast.27, f32[1,192]{1,0:T(1,128)} %bitcast.29), custom_call_target="tpu_custom_call" | custom-call | tf_op jit(solution)/shard_map/edges/pallas_call | solution.py:135
  2.5 0.1 collective-permute-start
  2.6 8.6 %collective-permute-start.1 = (f32[3,54,4,128]{3,2,1,0:T(4,128)S(1)}, f32[3,54,4,128]{3,2,1,0:T(4,128)S(1)}, u32[]{:S(2)}, u32[]{:S(2)}) collective-permute-start(f32[3,54,4,128]{3,2,1,0:T(4,128)S(1)} %get-tuple-element.58), channel_id=1, source_target_pairs={{0,248},{8,16},{16,8},{24,32},{32,24},{40,48},{48,40},{56,64},{64,... | collective-permute-start | bytes 995336 | tf_op jit(solution)/shard_map/ppermute | solution.py:613
  11.2 6.2 %prework.1 = (f32[3,36,4,192]{3,2,1,0:T(4,128)S(1)}, bf16[2,1920,192]{2,1,0:T(8,128)(2,1)S(1)}, bf16[2,640,384]{2,1,0:T(8,128)(2,1)S(1)}, bf16[2,192,1152]{2,1,0...) custom-call(f32[9,36,4,192]{3,2,1,0:T(4,128)} %bitcast.19, ...), custom_call_target="tpu_custom_call" | custom-call | tf_op jit(solution)/shard_map/prework/pallas_call | solution.py:220
  17.4 0.0 copy-start
  17.4 0.0 copy-start.1
  17.4 0.0 collective-permute-done.1.far
  17.4 0.4 columns.1
  17.9 0.9 %collective-permute-start.2 = (f32[15,3,4,192]{3,2,1,0:T(4,128)S(1)}, f32[15,3,4,192]{3,2,1,0:T(4,128)S(1)}, u32[]{:S(2)}, u32[]{:S(2)}) collective-permute-start(f32[15,3,4,192]{3,2,1,0:T(4,128)S(1)} %get-tuple-element.64), channel_id=1, source_target_pairs={{0,1},{1,0},{2,3},{3,2},{4,5},{5,4},{6,7},{7,6},{8,9},{9,8},{10,11... | collective-permute-start | bytes 414728 | tf_op jit(solution)/shard_map/ppermute | solution.py:614
  18.7 1.3 %collective-permute-start.3 = (f32[15,3,4,192]{3,2,1,0:T(4,128)S(1)}, f32[15,3,4,192]{3,2,1,0:T(4,128)S(1)}, u32[]{:S(2)}, u32[]{:S(2)}) collective-permute-start(f32[15,3,4,192]{3,2,1,0:T(4,128)S(1)} %get-tuple-element.65), channel_id=1, source_target_pairs={{0,7},{1,2},{2,1},{3,4},{4,3},{5,6},{6,5},{7,0},{8,15},{9,10},{10,... | collective-permute-start | bytes 414728 | tf_op jit(solution)/shard_map/ppermute | solution.py:613
  20.0 4.1 %core_columns.1 = (bf16[15,9,16,384]{3,2,1,0:T(8,128)(2,1)S(1)}, f32[15,3,16,192]{3,2,1,0:T(8,128)S(1)}, f32[15,3,16,192]{3,2,1,0:T(8,128)S(1)}, f32[15,15,16,19...) custom-call(s32[2,6]{1,0:T(2,128)S(1)} %bitcast.12, s32[2,6]{1,0:T(2,128)S(1)} %bitcast.15, ...), custom_call_target="tpu_custom_call" | custom-call | tf_op jit(solution)/shard_map/core_columns/pallas_call | solution.py:397
  24.1 2.3 %collective-permute-done.3.far_in = f32[15,3,4,192]{3,2,1,0:T(4,128)S(1)} collective-permute-done((f32[15,3,4,192]{3,2,1,0:T(4,128)S(1)}, f32[15,3,4,192]{3,2,1,0:T(4,128)S(1)}, u32[]{:S(2)}, u32[]{:S(2)}) %collective-permute-start.3) | collective-permute-done | bytes 138272 | tf_op jit(solution)/shard_map/ppermute | solution.py:613
  26.4 7.1 %outer_rows.1 = (f32[9,36,4,192]{3,2,1,0:T(4,128)}, f32[9,36,4,192]{3,2,1,0:T(4,128)}, f32[3,63,4,128]{3,2,1,0:T(4,128)S(1)}, f32[3,63,4,128]{3,2,1,0:T(4,128)S(...) custom-call(s32[2,6]{1,0:T(2,128)S(1)} %bitcast.13, s32[2,6]{1,0:T(2,128)S(1)} %bitcast.16, ...), custom_call_target="tpu_custom_call" | custom-call | tf_op jit(solution)/shard_map/outer_rows/pallas_call | solution.py:456
  33.5 0.1 collective-permute-start.4
  33.6 2.8 %collective-permute-start.5 = (f32[3,63,4,128]{3,2,1,0:T(4,128)S(1)}, f32[3,63,4,128]{3,2,1,0:T(4,128)S(1)}, u32[]{:S(2)}, u32[]{:S(2)}) collective-permute-start(f32[3,63,4,128]{3,2,1,0:T(4,128)S(1)} %get-tuple-element.92), channel_id=1, source_target_pairs={{0,248},{8,16},{16,8},{24,32},{32,24},{40,48},{48,40},{56,64},{64,... | collective-permute-start | bytes 1161224 | tf_op jit(solution)/shard_map/ppermute | solution.py:613
  36.4 6.1 %inner_rows.1 = (f32[9,36,4,192]{3,2,1,0:T(4,128)}, f32[9,36,4,192]{3,2,1,0:T(4,128)}, f32[9,9,16,192]{3,2,1,0:T(8,128)S(1)}, f32[9,3,4,192]{3,2,1,0:T(4,128)S(1...) custom-call(s32[2,6]{1,0:T(2,128)S(1)} %bitcast.14, ...), custom_call_target="tpu_custom_call", output_to_operand_aliasing={{0}: (2, {}), {1}: (3, {})} | custom-call | tf_op jit(solution)/shard_map/inner_rows/pallas_call | solution.py:513
  42.6 0.0 collective-permute-done.4.near
  42.6 2.1 %collective-permute-done.5.far = f32[3,63,4,128]{3,2,1,0:T(4,128)S(1)} collective-permute-done((f32[3,63,4,128]{3,2,1,0:T(4,128)S(1)}, f32[3,63,4,128]{3,2,1,0:T(4,128)S(1)}, u32[]{:S(2)}, u32[]{:S(2)}) %collective-permute-start.5) | collective-permute-done | bytes 387104 | tf_op jit(solution)/shard_map/ppermute | solution.py:613
  44.7 0.4 sums.1
  45.1 0.1 collective-permute-start.6
  45.2 1.4 %collective-permute-start.7 = (f32[9,3,4,192]{3,2,1,0:T(4,128)S(1)}, f32[9,3,4,192]{3,2,1,0:T(4,128)S(1)}, u32[]{:S(2)}, u32[]{:S(2)}) collective-permute-start(f32[9,3,4,192]{3,2,1,0:T(4,128)S(1)} %get-tuple-element.105), channel_id=1, source_target_pairs={{0,7},{1,2},{2,1},{3,4},{4,3},{5,6},{6,5},{7,0},{8,15},{9,10},{10,... | collective-permute-start | bytes 248840 | tf_op jit(solution)/shard_map/ppermute | solution.py:613
  46.6 3.7 %all_columns.1 = (f32[9,36,4,192]{3,2,1,0:T(4,128)}, f32[9,3,8,192]{3,2,1,0:T(8,128)S(1)}, f32[9,3,8,192]{3,2,1,0:T(8,128)S(1)}, f32[9,3,8,384]{3,2,1,0:T(8,128)S(1)}) custom-call(f32[3,42,4,192]{3,2,1,0:T(4,128)S(1)} %get-tuple-element.96.from_top, f32[3,42,4,192]{3,2,1,0:T(4,128)S(1)} %get-tuple-element.97.from_bottom, ...), custom_call_target="tpu_custom_call" | custom-call | tf_op jit(solution)/shard_map/all_columns/pallas_call | solution.py:563
  50.3 1.9 %collective-permute-done.7.far = f32[9,3,4,192]{3,2,1,0:T(4,128)S(1)} collective-permute-done((f32[9,3,4,192]{3,2,1,0:T(4,128)S(1)}, f32[9,3,4,192]{3,2,1,0:T(4,128)S(1)}, u32[]{:S(2)}, u32[]{:S(2)}) %collective-permute-start.7) | collective-permute-done | bytes 82976 | tf_op jit(solution)/shard_map/ppermute | solution.py:613
  52.2 1.6 %edge_columns.1 = f32[9,36,4,192]{3,2,1,0:T(4,128)} custom-call(f32[9,36,4,192]{3,2,1,0:T(4,128)} %get-tuple-element.103.out_in, f32[9,3,4,192]{3,2,1,0:T(4,128)S(1)} %collective-permute-done.6.near, f32[9,3,4,192]{3,2,1,0:T(4,128)S(1)} %collective-permute-done.7.far, ...), custom_call_target="tpu_custom_call", output_to_operand_aliasing={{}: (0, {})} | custom-call | tf_op jit(solution)/shard_map/edge_columns/pallas_call | solution.py:596
  (5 shorter events, 0.0 us)
Async XLA Ops:
  2.5 14.9 %collective-permute-start = (f32[3,54,4,128]{3,2,1,0:T(4,128)S(1)}, f32[3,54,4,128]{3,2,1,0:T(4,128)S(1)}, u32[]{:S(2)}, u32[]{:S(2)}) collective-permute-start(f32[3,54,4,128]{3,2,1,0:T(4,128)S(1)} %get-tuple-element.57), channel_id=1, source_target_pairs={{0,8},{8,0},{16,24},{24,16},{32,40},{40,32},{48,56},{56,48},{64,72... | collective-permute-start | bytes 995336 | tf_op jit(solution)/shard_map/ppermute | solution.py:614
  2.6 14.8 %collective-permute-start.1 = (f32[3,54,4,128]{3,2,1,0:T(4,128)S(1)}, f32[3,54,4,128]{3,2,1,0:T(4,128)S(1)}, u32[]{:S(2)}, u32[]{:S(2)}) collective-permute-start(f32[3,54,4,128]{3,2,1,0:T(4,128)S(1)} %get-tuple-element.58), channel_id=1, source_target_pairs={{0,248},{8,16},{16,8},{24,32},{32,24},{40,48},{48,40},{56,64},{64,... | collective-permute-start | bytes 995336 | tf_op jit(solution)/shard_map/ppermute | solution.py:613
  17.4 2.6 %copy-start = (s32[6,2]{0,1:T(2,128)S(1)}, s32[6,2]{0,1:T(2,128)}, u32[]{:S(2)}) copy-start(s32[6,2]{0,1:T(2,128)} %param.17) | copy-start | bytes 148
  17.4 2.6 %copy-start.1 = (s32[6,2]{0,1:T(2,128)S(1)}, s32[6,2]{0,1:T(2,128)}, u32[]{:S(2)}) copy-start(s32[6,2]{0,1:T(2,128)} %param.18) | copy-start | bytes 148
  17.9 6.2 %collective-permute-start.2 = (f32[15,3,4,192]{3,2,1,0:T(4,128)S(1)}, f32[15,3,4,192]{3,2,1,0:T(4,128)S(1)}, u32[]{:S(2)}, u32[]{:S(2)}) collective-permute-start(f32[15,3,4,192]{3,2,1,0:T(4,128)S(1)} %get-tuple-element.64), channel_id=1, source_target_pairs={{0,1},{1,0},{2,3},{3,2},{4,5},{5,4},{6,7},{7,6},{8,9},{9,8},{10,11... | collective-permute-start | bytes 414728 | tf_op jit(solution)/shard_map/ppermute | solution.py:614
  18.7 7.6 %collective-permute-start.3 = (f32[15,3,4,192]{3,2,1,0:T(4,128)S(1)}, f32[15,3,4,192]{3,2,1,0:T(4,128)S(1)}, u32[]{:S(2)}, u32[]{:S(2)}) collective-permute-start(f32[15,3,4,192]{3,2,1,0:T(4,128)S(1)} %get-tuple-element.65), channel_id=1, source_target_pairs={{0,7},{1,2},{2,1},{3,4},{4,3},{5,6},{6,5},{7,0},{8,15},{9,10},{10,... | collective-permute-start | bytes 414728 | tf_op jit(solution)/shard_map/ppermute | solution.py:613
  33.5 9.1 %collective-permute-start.4 = (f32[3,63,4,128]{3,2,1,0:T(4,128)S(1)}, f32[3,63,4,128]{3,2,1,0:T(4,128)S(1)}, u32[]{:S(2)}, u32[]{:S(2)}) collective-permute-start(f32[3,63,4,128]{3,2,1,0:T(4,128)S(1)} %get-tuple-element.91), channel_id=1, source_target_pairs={{0,8},{8,0},{16,24},{24,16},{32,40},{40,32},{48,56},{56,48},{64,72... | collective-permute-start | bytes 1161224 | tf_op jit(solution)/shard_map/ppermute | solution.py:614
  33.6 11.1 %collective-permute-start.5 = (f32[3,63,4,128]{3,2,1,0:T(4,128)S(1)}, f32[3,63,4,128]{3,2,1,0:T(4,128)S(1)}, u32[]{:S(2)}, u32[]{:S(2)}) collective-permute-start(f32[3,63,4,128]{3,2,1,0:T(4,128)S(1)} %get-tuple-element.92), channel_id=1, source_target_pairs={{0,248},{8,16},{16,8},{24,32},{32,24},{40,48},{48,40},{56,64},{64,... | collective-permute-start | bytes 1161224 | tf_op jit(solution)/shard_map/ppermute | solution.py:613
  45.1 5.1 %collective-permute-start.6 = (f32[9,3,4,192]{3,2,1,0:T(4,128)S(1)}, f32[9,3,4,192]{3,2,1,0:T(4,128)S(1)}, u32[]{:S(2)}, u32[]{:S(2)}) collective-permute-start(f32[9,3,4,192]{3,2,1,0:T(4,128)S(1)} %get-tuple-element.104), channel_id=1, source_target_pairs={{0,1},{1,0},{2,3},{3,2},{4,5},{5,4},{6,7},{7,6},{8,9},{9,8},{10,11... | collective-permute-start | bytes 248840 | tf_op jit(solution)/shard_map/ppermute | solution.py:614
  45.2 6.9 %collective-permute-start.7 = (f32[9,3,4,192]{3,2,1,0:T(4,128)S(1)}, f32[9,3,4,192]{3,2,1,0:T(4,128)S(1)}, u32[]{:S(2)}, u32[]{:S(2)}) collective-permute-start(f32[9,3,4,192]{3,2,1,0:T(4,128)S(1)} %get-tuple-element.105), channel_id=1, source_target_pairs={{0,7},{1,2},{2,1},{3,4},{4,3},{5,6},{6,5},{7,0},{8,15},{9,10},{10,... | collective-permute-start | bytes 248840 | tf_op jit(solution)/shard_map/ppermute | solution.py:613

commit v2 on v1

--- a/solution.py
+++ b/solution.py
@@ -86,11 +86,11 @@
     return (column == lane).astype(F32)
 
 
-def checks_row(check, syndrome, gain, pick):
+def gains_row(syndrome, gain, pick):
     bits = (2 * syndrome - 1).astype(F32)
     bits = jnp.concatenate([bits, bits], axis=0)
     sign = jnp.sum(pick * bits[None], axis=-1, keepdims=True)[:, 0:4, :]
-    return check + sign * gain
+    return sign * gain
 
 
 def is_odd(axis="gx"):
@@ -113,18 +113,18 @@
 
 def edges_kernel(check, syndrome, gain, far, near, first, last, rows, bits, gains, sems):
     copies = fetch(
-        [(syndrome, bits), (gain, gains)] + [(check.at[r], rows.at[r]) for r in (0, 1, 2, 6, 7, 8)], sems
+        [(syndrome, bits), (gain, gains)] + [(check.at[pl.ds(r, 3)], rows.at[pl.ds(r, 3)]) for r in (0, 6)], sems
     )
     pick = picker()
     copies[0].wait()
     copies[1].wait()
-    for n, r in enumerate((0, 1, 2, 6, 7, 8)):
-        copies[2 + n].wait()
-        value = checks_row(rows[r], bits[r], gains[...], pick)
-        if r < 3:
-            first[r] = value
-        else:
-            last[r - 6] = value
+    for r in range(3):
+        first[r] = gains_row(bits[r], gains[...], pick)
+        last[r] = gains_row(bits[6 + r], gains[...], pick)
+    copies[2].wait()
+    first[...] = first[...] + rows[0:3]
+    copies[3].wait()
+    last[...] = last[...] + rows[6:9]
     odd = is_odd() == 1
     low, high = dense(first[...]), dense(last[...])
     near[...] = jnp.where(odd, low, high)
@@ -139,7 +139,7 @@
         out_specs=vmem(4),
         scratch_shapes=[
             pltpu.VMEM((9, 36, 4, C), F32), pltpu.VMEM((9, 4, 36), jnp.int32), pltpu.VMEM((1, C), F32),
-            pltpu.SemaphoreType.DMA((8,)),
+            pltpu.SemaphoreType.DMA((4,)),
         ],
         name="edges",
         compiler_params=params(8),
@@ -160,7 +160,7 @@
 
 def prework_kernel(
     check, syndrome, gain, left, right, mix_one, grow_one, shrink_one, mix_two, first, last,
-    middle, m1, g1m, s1, m2, left_q, right_q, checks_q, left_g, right_g, center,
+    middle, m1, g1m, s1, m2, left_q, right_q, checks_q, left_g, right_g, pairs, acc,
     g1h, rows, bits, gains, lefts, rights, mix_1, grow_1, shrink_1, mix_2, sems,
 ):
     copies = fetch(
@@ -201,13 +201,14 @@
             copy.wait()
         pick = picker()
         for r in range(3):
-            middle[r] = checks_row(rows[r], bits[3 + r], gains[...], pick)
+            middle[r] = rows[r] + gains_row(bits[3 + r], gains[...], pick)
         for r, ref in enumerate((first, middle, last)):
             for q in range(4):
                 checks_q[3 * r : 3 * r + 3, :, 4 * q : 4 * q + 4, :] = ref[:, 9 * q : 9 * q + 9]
         tiles = packed(checks_q[...].reshape(1296, C))
         for t in range(3):
-            center[:, :, :, 128 * t : 128 * t + 128] = tiles[t].reshape(9, 9, 16, 128)
+            pairs[3:12, 3:12, :, 128 * t : 128 * t + 128] = tiles[t].reshape(9, 9, 16, 128)
+        acc[...] = jnp.zeros(acc.shape, F32)
 
     together(half(0, lefts, left_q, left_g), half(1, rights, right_q, right_g), checks())
 
@@ -222,9 +223,10 @@
         out_shape=results([(3, 36, 4, C)])
         + results(weights, BF16)
         + results(states)
-        + results([(9, 9, 16, 384)], BF16),
+        + results([(15, 15, 16, 384)], BF16)
+        + results([(15, 15, 16, C)]),
         in_specs=[HBM] * 9 + vmem(2),
-        out_specs=vmem(11),
+        out_specs=vmem(12),
         scratch_shapes=[pltpu.VMEM((2, 640, 384), BF16)]
         + [pltpu.VMEM(s, jnp.int32 if s == (9, 4, 36) else F32) for s in scratch]
         + [pltpu.SemaphoreType.DMA((9,))],
@@ -233,7 +235,7 @@
     )(*far_off(*operands[:9]), *operands[9:])
 
 
-def columns_kernel(first, middle, last, near, far, to_far, to_near, top, bottom, rows, low, high):
+def columns_kernel(near, far, first, middle, last, to_far, to_near, top, bottom, rows, low, high):
     undense(rows.at[0], near)
     undense(rows.at[1], far)
     odd = is_odd()
@@ -259,7 +261,7 @@
     )(*operands)
 
 
-def sums_kernel(acc_west, acc_east, near, far, to_far, to_near, top, bottom, rows, low, high):
+def sums_kernel(near, far, acc_west, acc_east, to_far, to_near, top, bottom, rows, low, high):
     undense(rows.at[0], near)
     undense(rows.at[1], far)
     odd = is_odd()
@@ -366,52 +368,54 @@
 
 
 def core_kernel(
-    off_one, off_two, first, middle, last, top, bottom, center, left_q, right_q, left_g, right_g, m1, g1m, s1, m2,
-    mid, west_q, east_q, acc, left_core, right_core,
+    off_one, off_two, pairs_in, acc_in, first, middle, last, top, bottom, left_q, right_q, left_g, right_g,
+    m1, g1m, s1, m2,
+    pairs, acc, west_q, east_q, left_core, right_core,
     field,
 ):
-    mid[3:12] = center[...]
     for at, ref in ((0, top), (12, bottom)):
         for q in range(4):
             field[:, :, 4 * q : 4 * q + 4, :] = ref[:, 9 * q : 9 * q + 9]
         tiles = packed(field[...].reshape(432, C))
         for t in range(3):
-            mid[at : at + 3, :, :, 128 * t : 128 * t + 128] = tiles[t].reshape(3, 9, 16, 128)
+            pairs[at : at + 3, 3:12, :, 128 * t : 128 * t + 128] = tiles[t].reshape(3, 9, 16, 128)
     for r, ref in enumerate((top, first, middle, last, bottom)):
         for q in range(3):
             east_q[3 * r : 3 * r + 3, :, 4 * q : 4 * q + 4, :] = ref[:, 9 * q + 9 : 9 * q + 12]
             west_q[3 * r : 3 * r + 3, :, 4 * q + 4 : 4 * q + 8, :] = ref[:, 9 * q + 6 : 9 * q + 9]
-    acc[...] = jnp.zeros(acc.shape, F32)
     news = layer_one_steps(
-        [(0, 3, 3), (6, 3, 3)], off_one, off_two, mid, 0, (left_q, right_q), (left_g, right_g), m1, g1m, s1, m2, acc,
-        SPAN,
+        [(0, 3, 3), (6, 3, 3)], off_one, off_two, pairs, SPAN, (left_q, right_q), (left_g, right_g), m1, g1m, s1, m2,
+        acc, SPAN,
     )
     for ref, (low, high) in zip((left_core, right_core), news):
         ref[0:3] = low
         ref[3:6] = high
 
 
+IN_PLACE = [(15, 15, 16, 384), (15, 15, 16, C)]
+
+
 def core_columns(off_one, off_two, *operands):
     smem = pl.BlockSpec(memory_space=pltpu.SMEM)
-    shapes = [(15, 3, 16, C), (15, 3, 16, C), (15, 15, 16, C), (6, 3, 16, C), (6, 3, 16, C)]
+    shapes = [(15, 3, 16, C), (15, 3, 16, C), (6, 3, 16, C), (6, 3, 16, C)]
     return pl.pallas_call(
         core_kernel,
-        out_shape=results([(15, 9, 16, 384)], BF16) + results(shapes),
-        in_specs=[smem, smem] + vmem(14),
+        out_shape=results(IN_PLACE[:1], BF16) + results(IN_PLACE[1:] + shapes),
+        in_specs=[smem, smem] + vmem(15),
         out_specs=vmem(6),
         scratch_shapes=[pltpu.VMEM((3, 9, 16, C), F32)],
+        input_output_aliases={2: 0, 3: 1},
         name="core_columns",
         compiler_params=params(12),
     )(off_one, off_two, *operands)
 
 
 def outer_kernel(
-    off_one, off_two, near_in, far_in, mid, west_q, east_q, acc_core, left_core, right_core,
+    off_one, off_two, pairs_in, acc_in, far_in, near_in, west_q, east_q, left_core, right_core,
     left_q, right_q, left_g, right_g, m1, g1m, s1, m2,
-    left_out, right_out, far, near, pairs, acc,
-    side, fresh, whole, sems,
+    pairs, acc, far, near, fresh,
+    side, whole,
 ):
-    pairs[:, 3:12] = mid[...]
     odd = is_odd("gy") == 1
     west = jnp.where(odd, near_in[...], far_in[...])
     east = jnp.where(odd, far_in[...], near_in[...])
@@ -421,22 +425,14 @@
         tiles = packed(side[...].reshape(720, C))
         for t in range(3):
             pairs[:, at : at + 3, :, 128 * t : 128 * t + 128] = tiles[t].reshape(15, 3, 16, 128)
-    acc[...] = acc_core[...]
     pieces = [(0, 0, 3), (0, 6, 3), (6, 0, 3), (6, 6, 3)]
     news = layer_one_steps(
         pieces, off_one, off_two, pairs, SPAN, (left_q, right_q), (left_g, right_g), m1, g1m, s1, m2, acc, SPAN
     )
-    copies = []
-    for b, (new, core, out) in enumerate(zip(news, (left_core, right_core), (left_out, right_out))):
+    for b, (new, core) in enumerate(zip(news, (left_core, right_core))):
         to_sites(fresh.at[b], core[...], 3)
         for (row, col, _), value in zip(pieces, new):
             to_sites(fresh.at[b, row // 2 : row // 2 + 3], value, col)
-        for i, at in enumerate((0, 6)):
-            copies.append(
-                pltpu.make_async_copy(fresh.at[b, pl.ds(3 * i, 3)], out.at[pl.ds(at, 3)], sems.at[2 * b + i])
-            )
-            copies[-1].start()
-
     for n, at in enumerate((0, 12)):
         rows = slice(at, at + 3)
         fold(acc, rows)
@@ -446,58 +442,50 @@
     odd = is_odd()
     near[...] = dense(whole[1 - odd])
     far[...] = dense(whole[odd])
-    for copy in copies:
-        copy.wait()
 
 
 def outer_rows(off_one, off_two, *operands):
-    states = [jax.ShapeDtypeStruct((9, 36, 4, C), F32)] * 2
     smem = pl.BlockSpec(memory_space=pltpu.SMEM)
+    shapes = [(3, 63, 4, 128), (3, 63, 4, 128), (2, 6, 36, 4, C)]
     return pl.pallas_call(
         outer_kernel,
-        out_shape=states
-        + results([(3, 63, 4, 128)] * 2)
-        + results([(15, 15, 16, 384)], BF16)
-        + results([(15, 15, 16, C)]),
+        out_shape=results(IN_PLACE[:1], BF16) + results(IN_PLACE[1:] + shapes),
         in_specs=[smem, smem] + vmem(16),
-        out_specs=[HBM] * 2 + vmem(4),
-        scratch_shapes=[
-            pltpu.VMEM((15, 3, 16, C), F32),
-            pltpu.VMEM((2, 6, 36, 4, C), F32),
-            pltpu.VMEM((2, 3, 42, 4, C), F32),
-            pltpu.SemaphoreType.DMA((4,)),
-        ],
+        out_specs=vmem(5),
+        scratch_shapes=[pltpu.VMEM((15, 3, 16, C), F32), pltpu.VMEM((2, 3, 42, 4, C), F32)],
+        input_output_aliases={2: 0, 3: 1},
         name="outer_rows",
-        compiler_params=params(18),
+        compiler_params=params(14),
     )(off_one, off_two, *operands)
 
 
 def inner_kernel(
-    off_one, off_two, left_in, right_in, grow_two, shrink_two, pairs, acc_in, center,
+    off_one, off_two, grow_two, shrink_two, pairs, acc_in, outer_states,
     left_q, right_q, left_g, right_g, m1, g1m, s1, m2,
     left_out, right_out, acc_mid, acc_west, acc_east, checks_g, g2m, s2,
     acc, fresh, grow_2, shrink_2, g2h, sems,
 ):
-    loads = [
-        pltpu.make_async_copy(src, dst, sems.at[2 + i])
-        for i, (src, dst) in enumerate(((grow_two, grow_2), (shrink_two, shrink_2)))
+    loads = fetch([(grow_two, grow_2), (shrink_two, shrink_2)], sems)
+    copies = [
+        pltpu.make_async_copy(outer_states.at[b, pl.ds(at // 2, 3)], out.at[pl.ds(at, 3)], sems.at[2 + 3 * b + n])
+        for b, out in enumerate((left_out, right_out))
+        for n, at in enumerate((0, 6))
     ]
-    for copy in loads:
+    for copy in copies:
         copy.start()
     acc[...] = acc_in[3:12]
-    copies = []
     news = layer_one_steps(
         [(3, 0, 9)], off_one, off_two, pairs, SPAN, (left_q, right_q), (left_g, right_g), m1, g1m, s1, m2, acc, 0
     )
     for b, ((new,), out) in enumerate(zip(news, (left_out, right_out))):
         to_sites(fresh.at[b], new)
-        copies.append(pltpu.make_async_copy(fresh.at[b], out.at[pl.ds(3, 3)], sems.at[b]))
-        copies[b].start()
+        copies.append(pltpu.make_async_copy(fresh.at[b], out.at[pl.ds(3, 3)], sems.at[4 + 3 * b]))
+        copies[-1].start()
     for copy in loads:
         copy.wait()
     grow(grow_2, g2h, g2m)
     shrink(shrink_2, s2)
-    tiles = center[...].reshape(1296, 384)
+    tiles = pairs[3:12, 3:12].reshape(1296, 384)
     checks_g[...] = dot(jnp.concatenate([tiles, tiles[:, :256]], axis=1), g2h[...]).reshape(9, 9, 16, 384)
     fold(acc, slice(0, 9))
     acc_mid[...] = acc[:, 3:12]
@@ -507,7 +495,7 @@
         copy.wait()
 
 
-def inner_rows(off_one, off_two, left_out, right_out, grow_two, shrink_two, *operands):
+def inner_rows(off_one, off_two, grow_two, shrink_two, *operands):
     states = [jax.ShapeDtypeStruct((9, 36, 4, C), F32)] * 2
     smem = pl.BlockSpec(memory_space=pltpu.SMEM)
     return pl.pallas_call(
@@ -515,7 +503,7 @@
         out_shape=states
         + results([(9, 9, 16, C), (9, 3, 4, C), (9, 3, 4, C), (9, 9, 16, 384)])
         + results([(640, 384), (C, 1152)], BF16),
-        in_specs=[smem, smem] + [HBM] * 4 + vmem(11),
+        in_specs=[smem, smem] + [HBM] * 2 + vmem(11),
         out_specs=[HBM] * 2 + vmem(6),
         scratch_shapes=[
             pltpu.VMEM((9, 15, 16, C), F32),
@@ -523,16 +511,15 @@
             pltpu.VMEM((384, 384), F32),
             pltpu.VMEM((C, 384), F32),
             pltpu.VMEM((640, 384), BF16),
-            pltpu.SemaphoreType.DMA((4,)),
+            pltpu.SemaphoreType.DMA((8,)),
         ],
-        input_output_aliases={2: 0, 3: 1},
         name="inner_rows",
         compiler_params=params(16),
-    )(off_one, off_two, left_out, right_out, *far_off(grow_two, shrink_two), *operands)
+    )(off_one, off_two, *far_off(grow_two, shrink_two), *operands)
 
 
 def all_columns_kernel(
-    from_top, from_bottom, acc_mid, checks_q, checks_g, g2m, s2, out, edge_m, edge_h, edge_g, acc, fresh, sems
+    from_top, from_bottom, acc_mid, checks_q, checks_g, g2m, s2, fresh, edge_m, edge_h, edge_g, acc
 ):
     acc[...] = acc_mid[...]
     for q in range(4):
@@ -550,31 +537,25 @@
             for r in groups
         )
     )
-    copies = []
-    for g, (rows, new) in enumerate(zip(groups, news)):
+    for rows, new in zip(groups, news):
         to_sites(fresh.at[rows], new.reshape(-1, 9, 16, C))
-        copies.append(pltpu.make_async_copy(fresh.at[rows], out.at[rows], sems.at[g]))
-        copies[g].start()
-    for copy in copies:
-        copy.wait()
 
 
 def all_columns(*operands):
     return pl.pallas_call(
         all_columns_kernel,
-        out_shape=[jax.ShapeDtypeStruct((9, 36, 4, C), F32)]
-        + results([(9, 3, 8, C), (9, 3, 8, C), (9, 3, 8, 384)]),
+        out_shape=results([(9, 36, 4, C), (9, 3, 8, C), (9, 3, 8, C), (9, 3, 8, 384)]),
         in_specs=vmem(7),
-        out_specs=[HBM] + vmem(3),
-        scratch_shapes=[
-            pltpu.VMEM((9, 9, 16, C), F32), pltpu.VMEM((9, 36, 4, C), F32), pltpu.SemaphoreType.DMA((2,)),
-        ],
+        out_specs=vmem(4),
+        scratch_shapes=[pltpu.VMEM((9, 9, 16, C), F32)],
         name="all_columns",
         compiler_params=params(14),
     )(*operands)
 
 
-def edge_columns_kernel(out_in, near, far, edge_m, edge_h, edge_g, g2m, s2, out, message, fresh, sems):
+def edge_columns_kernel(far, near, states, edge_m, edge_h, edge_g, g2m, s2, out, message, fresh, sems):
+    copies = [pltpu.make_async_copy(states.at[:, pl.ds(3, 30)], out.at[:, pl.ds(3, 30)], sems.at[2])]
+    copies[0].start()
     message[...] = edge_m[...]
     odd = is_odd("gy") == 1
     message[:, :, 0:4, :] = message[:, :, 0:4, :] + jnp.where(odd, near[...], far[...])
@@ -583,11 +564,10 @@
         update(edge_h[...].reshape(216, C), edge_g[...].reshape(216, 384), message[...].reshape(216, C), g2m, s2)
     )
     new = new.reshape(9, 3, 8, C)
-    copies = []
     for n, at in enumerate((0, 33)):
         fresh[n] = new[:, :, 4 * n : 4 * n + 4, :]
         copies.append(pltpu.make_async_copy(fresh.at[n], out.at[:, pl.ds(at, 3)], sems.at[n]))
-        copies[n].start()
+        copies[-1].start()
     for copy in copies:
         copy.wait()
 
@@ -596,12 +576,11 @@
     return pl.pallas_call(
         edge_columns_kernel,
         out_shape=jax.ShapeDtypeStruct((9, 36, 4, C), F32),
-        in_specs=[HBM] + vmem(7),
+        in_specs=vmem(8),
         out_specs=HBM,
         scratch_shapes=[
-            pltpu.VMEM((9, 3, 8, C), F32), pltpu.VMEM((2, 9, 3, 4, C), F32), pltpu.SemaphoreType.DMA((2,)),
+            pltpu.VMEM((9, 3, 8, C), F32), pltpu.VMEM((2, 9, 3, 4, C), F32), pltpu.SemaphoreType.DMA((3,)),
         ],
-        input_output_aliases={0: 0},
         name="edge_columns",
         compiler_params=params(8),
     )(*operands)
@@ -623,26 +602,26 @@
     check, bits, gain = site(check_state), jnp.transpose(syndrome, (1, 0, 2)), syndrome_gain.reshape(1, C)
     far, near, first, last = make_edges(check, bits, gain)
     near, far = trade(near, far, "gx")
-    middle, m1, g1m, s1, m2, left_q, right_q, checks_q, left_g, right_g, center = prework(
+    middle, m1, g1m, s1, m2, left_q, right_q, checks_q, left_g, right_g, pairs, acc = prework(
         check, bits, gain, site(left_state), site(right_state),
         mix_one, grow_one, jnp.swapaxes(shrink_one, 1, 2), mix_two, first, last,
     )
     near, far, middle = lax.optimization_barrier((near, far, middle))
-    far, near, top, bottom = make_columns(first, middle, last, near, far)
+    far, near, top, bottom = make_columns(near, far, first, middle, last)
     near, far = trade(near, far, "gy")
     steps = (offsets_one.T, offsets_two.T)
     shared = (left_q, right_q, left_g, right_g, m1, g1m, s1, m2)
-    core = core_columns(*steps, first, middle, last, top, bottom, center, *shared)
-    left_out, right_out, far, near, pairs, acc = outer_rows(*steps, near, far, *core, *shared)
+    pairs, acc, *core = core_columns(*steps, pairs, acc, first, middle, last, top, bottom, *shared)
+    pairs, acc, far, near, states = outer_rows(*steps, pairs, acc, far, near, *core, *shared)
     near, far = trade(near, far, "gx")
     left_out, right_out, acc_mid, acc_west, acc_east, checks_g, g2m, s2 = inner_rows(
-        *steps, left_out, right_out, grow_two, shrink_two.T, pairs, acc, center, *shared
+        *steps, grow_two, shrink_two.T, pairs, acc, states, *shared
     )
     near, far, acc_mid = lax.optimization_barrier((near, far, acc_mid))
-    far, near, from_top, from_bottom = make_sums(acc_west, acc_east, near, far)
+    far, near, from_top, from_bottom = make_sums(near, far, acc_west, acc_east)
     near, far = trade(near, far, "gy")
-    check_out, edge_m, edge_h, edge_g = all_columns(from_top, from_bottom, acc_mid, checks_q, checks_g, g2m, s2)
-    check_out = edge_columns(check_out, near, far, edge_m, edge_h, edge_g, g2m, s2)
+    states, edge_m, edge_h, edge_g = all_columns(from_top, from_bottom, acc_mid, checks_q, checks_g, g2m, s2)
+    check_out = edge_columns(far, near, states, edge_m, edge_h, edge_g, g2m, s2)
     return back(left_out), back(right_out), back(check_out)
 
 

time: 54 us -> 52.8 us (0.978)
  Pallas kernels: 31.5 us -> 29.4 us
    pallas_call x3, Pallas kernels: 14.9 us -> 13 us  [the longest x1 6.59 us: outer_rows(): pl.pallas_call(outer_kernel, out_shape=results(IN_PLACE[:1], BF16) + resu...]
  transfers between devices with their start and end apart: 8 -> 8, of which waited for: 3 -> 3; matrix products, arithmetic and copies ran while one was open for 0% -> 0% of each run, Pallas kernels for 37% -> 36%
where the time goes in v2:
time: 52.8 us; the launch traced here: 52.2 us
  Pallas kernels  29.4 us (56%)
  starting transfers between devices  15.3 us (29%)
  waiting for transfers between devices  6.62 us (13%)
  between operations  0.93 us (2%)
    ppermute x4, starting transfers between devices, trade(): got = lax.ppermute(far, axis, beyond)  14.3 us
    ppermute x4, waiting for transfers between devices, trade(): got = lax.ppermute(far, axis, beyond)  6.61 us
    pallas_call x1, Pallas kernels, outer_rows(): pl.pallas_call(outer_kernel, out_shape=results(IN_PLACE[:1], BF16) + resu...  6.59 us
    pallas_call x1, Pallas kernels, prework(): pl.pallas_call(prework_kernel, out_shape=results([(3, 36, 4, C)]) + resul...  6.31 us
    pallas_call x1, Pallas kernels, inner_rows(): pl.pallas_call(inner_kernel, out_shape=states + results([(9, 9, 16, C), (...  6.19 us
    pallas_call x1, Pallas kernels, core_columns(): pl.pallas_call(core_kernel, out_shape=results(IN_PLACE[:1], BF16) + resul...  3.77 us
    pallas_call x1, Pallas kernels, all_columns(): pl.pallas_call(all_columns_kernel, out_shape=results([(9, 36, 4, C), (9,...  2.6 us
    pallas_call x1, Pallas kernels, edge_columns(): pl.pallas_call(edge_columns_kernel, out_shape=jax.ShapeDtypeStruct((9, 36...  1.58 us
  transfers between devices with their start and end apart: 8, of which 3 were waited for; matrix products, arithmetic and copies ran while one was open for 0% of the time, Pallas kernels for 36%

profile of v2, /device:TPU:6, one launch (start us, length us, event | category | flops | bytes accessed | tf_op | source)
XLA Modules:
  0.0 52.2 jit_solution(10003630425035554639)
XLA Ops:
  0.6 1.4 %edges.1 = (f32[3,54,4,128]{3,2,1,0:T(4,128)S(1)}, f32[3,54,4,128]{3,2,1,0:T(4,128)S(1)}, f32[3,36,4,192]{3,2,1,0:T(4,128)S(1)}, f32[3,36,4,192]{3,2,1,0:T(4,128)S(1)}) custom-call(f32[9,36,4,192]{3,2,1,0:T(4,128)} %bitcast.18, s32[9,4,36]{2,1,0:T(4,128)} %bitcast.25, f32[1,192]{1,0:T(1,128)} %bitcast.27), custom_call_target="tpu_custom_call" | custom-call | tf_op jit(solution)/shard_map/edges/pallas_call | solution.py:135
  2.1 0.1 collective-permute-start
  2.2 8.6 %collective-permute-start.1 = (f32[3,54,4,128]{3,2,1,0:T(4,128)S(1)}, f32[3,54,4,128]{3,2,1,0:T(4,128)S(1)}, u32[]{:S(2)}, u32[]{:S(2)}) collective-permute-start(f32[3,54,4,128]{3,2,1,0:T(4,128)S(1)} %get-tuple-element.61), channel_id=1, source_target_pairs={{0,248},{8,16},{16,8},{24,32},{32,24},{40,48},{48,40},{56,64},{64,... | collective-permute-start | bytes 995336 | tf_op jit(solution)/shard_map/ppermute | solution.py:592
  10.8 6.3 %prework.1 = (f32[3,36,4,192]{3,2,1,0:T(4,128)S(1)}, bf16[2,1920,192]{2,1,0:T(8,128)(2,1)S(1)}, bf16[2,640,384]{2,1,0:T(8,128)(2,1)S(1)}, bf16[2,192,1152]{2,1,0...) custom-call(f32[9,36,4,192]{3,2,1,0:T(4,128)} %bitcast.19, ...), custom_call_target="tpu_custom_call" | custom-call | tf_op jit(solution)/shard_map/prework/pallas_call | solution.py:221
  17.1 0.0 copy-start
  17.1 0.0 copy-start.1
  17.1 0.0 collective-permute-done.near
  17.1 0.0 collective-permute-done.1.far
  17.1 0.4 columns.1
  17.6 0.7 %collective-permute-start.2 = (f32[15,3,4,192]{3,2,1,0:T(4,128)S(1)}, f32[15,3,4,192]{3,2,1,0:T(4,128)S(1)}, u32[]{:S(2)}, u32[]{:S(2)}) collective-permute-start(f32[15,3,4,192]{3,2,1,0:T(4,128)S(1)} %get-tuple-element.78), channel_id=1, source_target_pairs={{0,7},{1,2},{2,1},{3,4},{4,3},{5,6},{6,5},{7,0},{8,15},{9,10},{10,... | collective-permute-start | bytes 414728 | tf_op jit(solution)/shard_map/ppermute | solution.py:592
  18.2 0.8 %collective-permute-start.3 = (f32[15,3,4,192]{3,2,1,0:T(4,128)S(1)}, f32[15,3,4,192]{3,2,1,0:T(4,128)S(1)}, u32[]{:S(2)}, u32[]{:S(2)}) collective-permute-start(f32[15,3,4,192]{3,2,1,0:T(4,128)S(1)} %get-tuple-element.79), channel_id=1, source_target_pairs={{0,1},{1,0},{2,3},{3,2},{4,5},{5,4},{6,7},{7,6},{8,9},{9,8},{10,11... | collective-permute-start | bytes 414728 | tf_op jit(solution)/shard_map/ppermute | solution.py:593
  19.0 3.8 %core_columns.1 = (bf16[15,15,16,384]{3,2,1,0:T(8,128)(2,1)S(1)}, f32[15,15,16,192]{3,2,1,0:T(8,128)S(1)}, f32[15,3,16,192]{3,2,1,0:T(8,128)S(1)}, f32[15,3,16,1...) custom-call(s32[2,6]{1,0:T(2,128)S(1)} %bitcast.12, ...), custom_call_target="tpu_custom_call", output_to_operand_aliasing={{0}: (2, {}), {1}: (3, {})} | custom-call | tf_op jit(solution)/shard_map/core_columns/pallas_call | solution.py:401
  22.8 2.5 %collective-permute-done.2.far_in = f32[15,3,4,192]{3,2,1,0:T(4,128)S(1)} collective-permute-done((f32[15,3,4,192]{3,2,1,0:T(4,128)S(1)}, f32[15,3,4,192]{3,2,1,0:T(4,128)S(1)}, u32[]{:S(2)}, u32[]{:S(2)}) %collective-permute-start.2) | collective-permute-done | bytes 138272 | tf_op jit(solution)/shard_map/ppermute | solution.py:592
  25.3 0.0 collective-permute-done.3.near_in
  25.3 6.6 %outer_rows.1 = (bf16[15,15,16,384]{3,2,1,0:T(8,128)(2,1)S(1)}, f32[15,15,16,192]{3,2,1,0:T(8,128)S(1)}, f32[3,63,4,128]{3,2,1,0:T(4,128)S(1)}, f32[3,63,4,128]{3,2,1,0:T(4,128)S(1)}, f32[2,6,36,4,192]{4,3,2,1,0:T(4,128)S(1)}) custom-call(s32[2,6]{1,0:T(2,128)S(1)} %bitcast.13, s32[2,6]{1,0:T(2,128)S(1)} %bitcast.16, ...), custom_call_target="tpu_custom_call", output_to_operand_aliasing={{0}: (2, {}), {1}: (3, {})} | custom-call | tf_op jit(solution)/shard_map/outer_rows/pallas_call | solution.py:450
  31.9 0.1 collective-permute-start.4
  32.0 3.0 %collective-permute-start.5 = (f32[3,63,4,128]{3,2,1,0:T(4,128)S(1)}, f32[3,63,4,128]{3,2,1,0:T(4,128)S(1)}, u32[]{:S(2)}, u32[]{:S(2)}) collective-permute-start(f32[3,63,4,128]{3,2,1,0:T(4,128)S(1)} %get-tuple-element.90), channel_id=1, source_target_pairs={{0,248},{8,16},{16,8},{24,32},{32,24},{40,48},{48,40},{56,64},{64,... | collective-permute-start | bytes 1161224 | tf_op jit(solution)/shard_map/ppermute | solution.py:592
  34.9 6.2 %inner_rows.1 = (f32[9,36,4,192]{3,2,1,0:T(4,128)}, f32[9,36,4,192]{3,2,1,0:T(4,128)}, f32[9,9,16,192]{3,2,1,0:T(8,128)S(1)}, f32[9,3,4,192]{3,2,1,0:T(4,128)S(1...) custom-call(s32[2,6]{1,0:T(2,128)S(1)} %bitcast.14, ...), custom_call_target="tpu_custom_call" | custom-call | tf_op jit(solution)/shard_map/inner_rows/pallas_call | solution.py:501
  41.2 1.9 %collective-permute-done.5.far = f32[3,63,4,128]{3,2,1,0:T(4,128)S(1)} collective-permute-done((f32[3,63,4,128]{3,2,1,0:T(4,128)S(1)}, f32[3,63,4,128]{3,2,1,0:T(4,128)S(1)}, u32[]{:S(2)}, u32[]{:S(2)}) %collective-permute-start.5) | collective-permute-done | bytes 387104 | tf_op jit(solution)/shard_map/ppermute | solution.py:592
  43.1 0.4 sums.1
  43.5 2.1 %collective-permute-start.6 = (f32[9,3,4,192]{3,2,1,0:T(4,128)S(1)}, f32[9,3,4,192]{3,2,1,0:T(4,128)S(1)}, u32[]{:S(2)}, u32[]{:S(2)}) collective-permute-start(f32[9,3,4,192]{3,2,1,0:T(4,128)S(1)} %get-tuple-element.96), channel_id=1, source_target_pairs={{0,7},{1,2},{2,1},{3,4},{4,3},{5,6},{6,5},{7,0},{8,15},{9,10},{10,... | collective-permute-start | bytes 248840 | tf_op jit(solution)/shard_map/ppermute | solution.py:592
  45.6 2.6 %all_columns.1 = (f32[9,36,4,192]{3,2,1,0:T(4,128)S(1)}, f32[9,3,8,192]{3,2,1,0:T(8,128)S(1)}, f32[9,3,8,192]{3,2,1,0:T(8,128)S(1)}, f32[9,3,8,384]{3,2,1,0:T(8,128)S(1)}) custom-call(f32[3,42,4,192]{3,2,1,0:T(4,128)S(1)} %get-tuple-element.98.from_top, f32[3,42,4,192]{3,2,1,0:T(4,128)S(1)} %get-tuple-element.99.from_bottom, ...), custom_call_target="tpu_custom_call" | custom-call | tf_op jit(solution)/shard_map/all_columns/pallas_call | solution.py:545
  48.2 2.2 %collective-permute-done.6.far = f32[9,3,4,192]{3,2,1,0:T(4,128)S(1)} collective-permute-done((f32[9,3,4,192]{3,2,1,0:T(4,128)S(1)}, f32[9,3,4,192]{3,2,1,0:T(4,128)S(1)}, u32[]{:S(2)}, u32[]{:S(2)}) %collective-permute-start.6) | collective-permute-done | bytes 82976 | tf_op jit(solution)/shard_map/ppermute | solution.py:592
  50.5 1.6 %edge_columns.1 = f32[9,36,4,192]{3,2,1,0:T(4,128)} custom-call(f32[9,3,4,192]{3,2,1,0:T(4,128)S(1)} %collective-permute-done.6.far, f32[9,3,4,192]{3,2,1,0:T(4,128)S(1)} %collective-permute-done.7.near, f32[9,36,4,192]{3,2,1,0:T(4,128)S(1)} %get-tuple-element.105.states, f32[9,3,8,192]{3,2,1,0:T(8,128)S(1)} %get-tuple-element.106.edge_m, ...), custom_call_target="tpu_custom_call" | custom-call | tf_op jit(solution)/shard_map/edge_columns/pallas_call | solution.py:576
  (5 shorter events, 0.0 us)
Async XLA Ops:
  2.1 15.0 %collective-permute-start = (f32[3,54,4,128]{3,2,1,0:T(4,128)S(1)}, f32[3,54,4,128]{3,2,1,0:T(4,128)S(1)}, u32[]{:S(2)}, u32[]{:S(2)}) collective-permute-start(f32[3,54,4,128]{3,2,1,0:T(4,128)S(1)} %get-tuple-element.60), channel_id=1, source_target_pairs={{0,8},{8,0},{16,24},{24,16},{32,40},{40,32},{48,56},{56,48},{64,72... | collective-permute-start | bytes 995336 | tf_op jit(solution)/shard_map/ppermute | solution.py:593
  2.2 14.9 %collective-permute-start.1 = (f32[3,54,4,128]{3,2,1,0:T(4,128)S(1)}, f32[3,54,4,128]{3,2,1,0:T(4,128)S(1)}, u32[]{:S(2)}, u32[]{:S(2)}) collective-permute-start(f32[3,54,4,128]{3,2,1,0:T(4,128)S(1)} %get-tuple-element.61), channel_id=1, source_target_pairs={{0,248},{8,16},{16,8},{24,32},{32,24},{40,48},{48,40},{56,64},{64,... | collective-permute-start | bytes 995336 | tf_op jit(solution)/shard_map/ppermute | solution.py:592
  17.1 1.9 %copy-start = (s32[6,2]{0,1:T(2,128)S(1)}, s32[6,2]{0,1:T(2,128)}, u32[]{:S(2)}) copy-start(s32[6,2]{0,1:T(2,128)} %param.17) | copy-start | bytes 148
  17.1 1.9 %copy-start.1 = (s32[6,2]{0,1:T(2,128)S(1)}, s32[6,2]{0,1:T(2,128)}, u32[]{:S(2)}) copy-start(s32[6,2]{0,1:T(2,128)} %param.18) | copy-start | bytes 148
  17.6 7.7 %collective-permute-start.2 = (f32[15,3,4,192]{3,2,1,0:T(4,128)S(1)}, f32[15,3,4,192]{3,2,1,0:T(4,128)S(1)}, u32[]{:S(2)}, u32[]{:S(2)}) collective-permute-start(f32[15,3,4,192]{3,2,1,0:T(4,128)S(1)} %get-tuple-element.78), channel_id=1, source_target_pairs={{0,7},{1,2},{2,1},{3,4},{4,3},{5,6},{6,5},{7,0},{8,15},{9,10},{10,... | collective-permute-start | bytes 414728 | tf_op jit(solution)/shard_map/ppermute | solution.py:592
  18.2 7.1 %collective-permute-start.3 = (f32[15,3,4,192]{3,2,1,0:T(4,128)S(1)}, f32[15,3,4,192]{3,2,1,0:T(4,128)S(1)}, u32[]{:S(2)}, u32[]{:S(2)}) collective-permute-start(f32[15,3,4,192]{3,2,1,0:T(4,128)S(1)} %get-tuple-element.79), channel_id=1, source_target_pairs={{0,1},{1,0},{2,3},{3,2},{4,5},{5,4},{6,7},{7,6},{8,9},{9,8},{10,11... | collective-permute-start | bytes 414728 | tf_op jit(solution)/shard_map/ppermute | solution.py:593
  31.9 9.3 %collective-permute-start.4 = (f32[3,63,4,128]{3,2,1,0:T(4,128)S(1)}, f32[3,63,4,128]{3,2,1,0:T(4,128)S(1)}, u32[]{:S(2)}, u32[]{:S(2)}) collective-permute-start(f32[3,63,4,128]{3,2,1,0:T(4,128)S(1)} %get-tuple-element.89), channel_id=1, source_target_pairs={{0,8},{8,0},{16,24},{24,16},{32,40},{40,32},{48,56},{56,48},{64,72... | collective-permute-start | bytes 1161224 | tf_op jit(solution)/shard_map/ppermute | solution.py:593
  32.0 11.1 %collective-permute-start.5 = (f32[3,63,4,128]{3,2,1,0:T(4,128)S(1)}, f32[3,63,4,128]{3,2,1,0:T(4,128)S(1)}, u32[]{:S(2)}, u32[]{:S(2)}) collective-permute-start(f32[3,63,4,128]{3,2,1,0:T(4,128)S(1)} %get-tuple-element.90), channel_id=1, source_target_pairs={{0,248},{8,16},{16,8},{24,32},{32,24},{40,48},{48,40},{56,64},{64,... | collective-permute-start | bytes 1161224 | tf_op jit(solution)/shard_map/ppermute | solution.py:592
  43.5 6.9 %collective-permute-start.6 = (f32[9,3,4,192]{3,2,1,0:T(4,128)S(1)}, f32[9,3,4,192]{3,2,1,0:T(4,128)S(1)}, u32[]{:S(2)}, u32[]{:S(2)}) collective-permute-start(f32[9,3,4,192]{3,2,1,0:T(4,128)S(1)} %get-tuple-element.96), channel_id=1, source_target_pairs={{0,7},{1,2},{2,1},{3,4},{4,3},{5,6},{6,5},{7,0},{8,15},{9,10},{10,... | collective-permute-start | bytes 248840 | tf_op jit(solution)/shard_map/ppermute | solution.py:592
  45.6 4.8 %collective-permute-start.7 = (f32[9,3,4,192]{3,2,1,0:T(4,128)S(1)}, f32[9,3,4,192]{3,2,1,0:T(4,128)S(1)}, u32[]{:S(2)}, u32[]{:S(2)}) collective-permute-start(f32[9,3,4,192]{3,2,1,0:T(4,128)S(1)} %get-tuple-element.97), channel_id=1, source_target_pairs={{0,1},{1,0},{2,3},{3,2},{4,5},{5,4},{6,7},{7,6},{8,9},{9,8},{10,11... | collective-permute-start | bytes 248840 | tf_op jit(solution)/shard_map/ppermute | solution.py:593

commit v3 on v2

--- a/solution.py
+++ b/solution.py
@@ -235,12 +235,11 @@
     )(*far_off(*operands[:9]), *operands[9:])
 
 
-def columns_kernel(near, far, first, middle, last, to_far, to_near, top, bottom, rows, low, high):
-    undense(rows.at[0], near)
-    undense(rows.at[1], far)
+def columns_kernel(near, far, first, middle, last, to_far, to_near, beyond, low, high):
     odd = is_odd()
-    top[...] = rows[1 - odd]
-    bottom[...] = rows[odd]
+    undense(beyond.at[1 - odd], near)
+    undense(beyond.at[odd], far)
+    top, bottom = beyond.at[0], beyond.at[1]
     for r, ref in enumerate((top, first, middle, last, bottom)):
         low[3 * r : 3 * r + 3] = ref[:, 0:3]
         high[3 * r : 3 * r + 3] = ref[:, 33:36]
@@ -252,21 +251,20 @@
 def make_columns(*operands):
     return pl.pallas_call(
         columns_kernel,
-        out_shape=results([(15, 3, 4, C)] * 2 + [(3, 36, 4, C)] * 2),
+        out_shape=results([(15, 3, 4, C)] * 2 + [(2, 3, 36, 4, C)]),
         in_specs=vmem(5),
-        out_specs=vmem(4),
-        scratch_shapes=[pltpu.VMEM((2, 3, 36, 4, C), F32)] + [pltpu.VMEM((15, 3, 4, C), F32)] * 2,
+        out_specs=vmem(3),
+        scratch_shapes=[pltpu.VMEM((15, 3, 4, C), F32)] * 2,
         name="columns",
         compiler_params=params(6),
     )(*operands)
 
 
-def sums_kernel(near, far, acc_west, acc_east, to_far, to_near, top, bottom, rows, low, high):
-    undense(rows.at[0], near)
-    undense(rows.at[1], far)
+def sums_kernel(near, far, acc_west, acc_east, to_far, to_near, beyond, low, high):
     odd = is_odd()
-    top[...] = rows[1 - odd]
-    bottom[...] = rows[odd]
+    undense(beyond.at[1 - odd], near)
+    undense(beyond.at[odd], far)
+    top, bottom = beyond.at[0], beyond.at[1]
     for ref, acc, cols in ((low, acc_west, slice(0, 3)), (high, acc_east, slice(39, 42))):
         ref[0:3] = acc[0:3] + top[:, cols]
         ref[3:6] = acc[3:6]
@@ -279,10 +277,10 @@
 def make_sums(*operands):
     return pl.pallas_call(
         sums_kernel,
-        out_shape=results([(9, 3, 4, C)] * 2 + [(3, 42, 4, C)] * 2),
+        out_shape=results([(9, 3, 4, C)] * 2 + [(2, 3, 42, 4, C)]),
         in_specs=vmem(4),
-        out_specs=vmem(4),
-        scratch_shapes=[pltpu.VMEM((2, 3, 42, 4, C), F32)] + [pltpu.VMEM((9, 3, 4, C), F32)] * 2,
+        out_specs=vmem(3),
+        scratch_shapes=[pltpu.VMEM((9, 3, 4, C), F32)] * 2,
         name="sums",
         compiler_params=params(6),
     )(*operands)
@@ -368,11 +366,12 @@
 
 
 def core_kernel(
-    off_one, off_two, pairs_in, acc_in, first, middle, last, top, bottom, left_q, right_q, left_g, right_g,
+    off_one, off_two, pairs_in, acc_in, first, middle, last, beyond, left_q, right_q, left_g, right_g,
     m1, g1m, s1, m2,
     pairs, acc, west_q, east_q, left_core, right_core,
     field,
 ):
+    top, bottom = beyond.at[0], beyond.at[1]
     for at, ref in ((0, top), (12, bottom)):
         for q in range(4):
             field[:, :, 4 * q : 4 * q + 4, :] = ref[:, 9 * q : 9 * q + 9]
@@ -401,7 +400,7 @@
     return pl.pallas_call(
         core_kernel,
         out_shape=results(IN_PLACE[:1], BF16) + results(IN_PLACE[1:] + shapes),
-        in_specs=[smem, smem] + vmem(15),
+        in_specs=[smem, smem] + vmem(14),
         out_specs=vmem(6),
         scratch_shapes=[pltpu.VMEM((3, 9, 16, C), F32)],
         input_output_aliases={2: 0, 3: 1},
@@ -519,8 +518,9 @@
 
 
 def all_columns_kernel(
-    from_top, from_bottom, acc_mid, checks_q, checks_g, g2m, s2, fresh, edge_m, edge_h, edge_g, acc
+    beyond, acc_mid, checks_q, checks_g, g2m, s2, fresh, edge_m, edge_h, edge_g, acc
 ):
+    from_top, from_bottom = beyond.at[0], beyond.at[1]
     acc[...] = acc_mid[...]
     for q in range(4):
         sub = slice(4 * q, 4 * q + 4)
@@ -545,7 +545,7 @@
     return pl.pallas_call(
         all_columns_kernel,
         out_shape=results([(9, 36, 4, C), (9, 3, 8, C), (9, 3, 8, C), (9, 3, 8, 384)]),
-        in_specs=vmem(7),
+        in_specs=vmem(6),
         out_specs=vmem(4),
         scratch_shapes=[pltpu.VMEM((9, 9, 16, C), F32)],
         name="all_columns",
@@ -607,20 +607,20 @@
         mix_one, grow_one, jnp.swapaxes(shrink_one, 1, 2), mix_two, first, last,
     )
     near, far, middle = lax.optimization_barrier((near, far, middle))
-    far, near, top, bottom = make_columns(near, far, first, middle, last)
+    far, near, rows = make_columns(near, far, first, middle, last)
     near, far = trade(near, far, "gy")
     steps = (offsets_one.T, offsets_two.T)
     shared = (left_q, right_q, left_g, right_g, m1, g1m, s1, m2)
-    pairs, acc, *core = core_columns(*steps, pairs, acc, first, middle, last, top, bottom, *shared)
+    pairs, acc, *core = core_columns(*steps, pairs, acc, first, middle, last, rows, *shared)
     pairs, acc, far, near, states = outer_rows(*steps, pairs, acc, far, near, *core, *shared)
     near, far = trade(near, far, "gx")
     left_out, right_out, acc_mid, acc_west, acc_east, checks_g, g2m, s2 = inner_rows(
         *steps, grow_two, shrink_two.T, pairs, acc, states, *shared
     )
     near, far, acc_mid = lax.optimization_barrier((near, far, acc_mid))
-    far, near, from_top, from_bottom = make_sums(near, far, acc_west, acc_east)
+    far, near, rows = make_sums(near, far, acc_west, acc_east)
     near, far = trade(near, far, "gy")
-    states, edge_m, edge_h, edge_g = all_columns(from_top, from_bottom, acc_mid, checks_q, checks_g, g2m, s2)
+    states, edge_m, edge_h, edge_g = all_columns(rows, acc_mid, checks_q, checks_g, g2m, s2)
     check_out = edge_columns(far, near, states, edge_m, edge_h, edge_g, g2m, s2)
     return back(left_out), back(right_out), back(check_out)
 

time: 52.8 us -> 52.6 us (level)
  no operation moved by 1% of the time
where the time goes in v3:
time: 52.6 us; the launch traced here: 52 us
  Pallas kernels  29.1 us (55%)
  starting transfers between devices  15.3 us (29%)
  waiting for transfers between devices  6.63 us (13%)
  between operations  0.93 us (2%)
    ppermute x4, starting transfers between devices, trade(): got = lax.ppermute(far, axis, beyond)  14.3 us
    ppermute x4, waiting for transfers between devices, trade(): got = lax.ppermute(far, axis, beyond)  6.62 us
    pallas_call x1, Pallas kernels, outer_rows(): pl.pallas_call(outer_kernel, out_shape=results(IN_PLACE[:1], BF16) + resu...  6.59 us
    pallas_call x1, Pallas kernels, prework(): pl.pallas_call(prework_kernel, out_shape=results([(3, 36, 4, C)]) + resul...  6.31 us
    pallas_call x1, Pallas kernels, inner_rows(): pl.pallas_call(inner_kernel, out_shape=states + results([(9, 9, 16, C), (...  6.19 us
    pallas_call x1, Pallas kernels, core_columns(): pl.pallas_call(core_kernel, out_shape=results(IN_PLACE[:1], BF16) + resul...  3.76 us
    pallas_call x1, Pallas kernels, all_columns(): pl.pallas_call(all_columns_kernel, out_shape=results([(9, 36, 4, C), (9,...  2.61 us
    pallas_call x1, Pallas kernels, edge_columns(): pl.pallas_call(edge_columns_kernel, out_shape=jax.ShapeDtypeStruct((9, 36...  1.58 us
  transfers between devices with their start and end apart: 8, of which 3 were waited for; matrix products, arithmetic and copies ran while one was open for 0% of the time, Pallas kernels for 36%

profile of v3, /device:TPU:6, one launch (start us, length us, event | category | flops | bytes accessed | tf_op | source)
XLA Modules:
  0.0 52.0 jit_solution(2578522218008846303)
XLA Ops:
  0.6 1.4 %edges.1 = (f32[3,54,4,128]{3,2,1,0:T(4,128)S(1)}, f32[3,54,4,128]{3,2,1,0:T(4,128)S(1)}, f32[3,36,4,192]{3,2,1,0:T(4,128)S(1)}, f32[3,36,4,192]{3,2,1,0:T(4,128)S(1)}) custom-call(f32[9,36,4,192]{3,2,1,0:T(4,128)} %bitcast.18, s32[9,4,36]{2,1,0:T(4,128)} %bitcast.25, f32[1,192]{1,0:T(1,128)} %bitcast.27), custom_call_target="tpu_custom_call" | custom-call | tf_op jit(solution)/shard_map/edges/pallas_call | solution.py:135
  2.1 0.1 collective-permute-start
  2.2 8.6 %collective-permute-start.1 = (f32[3,54,4,128]{3,2,1,0:T(4,128)S(1)}, f32[3,54,4,128]{3,2,1,0:T(4,128)S(1)}, u32[]{:S(2)}, u32[]{:S(2)}) collective-permute-start(f32[3,54,4,128]{3,2,1,0:T(4,128)S(1)} %get-tuple-element.59), channel_id=1, source_target_pairs={{0,248},{8,16},{16,8},{24,32},{32,24},{40,48},{48,40},{56,64},{64,... | collective-permute-start | bytes 995336 | tf_op jit(solution)/shard_map/ppermute | solution.py:592
  10.8 6.3 %prework.1 = (f32[3,36,4,192]{3,2,1,0:T(4,128)S(1)}, bf16[2,1920,192]{2,1,0:T(8,128)(2,1)S(1)}, bf16[2,640,384]{2,1,0:T(8,128)(2,1)S(1)}, bf16[2,192,1152]{2,1,0...) custom-call(f32[9,36,4,192]{3,2,1,0:T(4,128)} %bitcast.19, ...), custom_call_target="tpu_custom_call" | custom-call | tf_op jit(solution)/shard_map/prework/pallas_call | solution.py:221
  17.1 0.0 copy-start
  17.1 0.0 copy-start.1
  17.1 0.0 collective-permute-done.near
  17.1 0.0 collective-permute-done.1.far
  17.1 0.3 columns.1
  17.4 0.7 %collective-permute-start.2 = (f32[15,3,4,192]{3,2,1,0:T(4,128)S(1)}, f32[15,3,4,192]{3,2,1,0:T(4,128)S(1)}, u32[]{:S(2)}, u32[]{:S(2)}) collective-permute-start(f32[15,3,4,192]{3,2,1,0:T(4,128)S(1)} %get-tuple-element.75), channel_id=1, source_target_pairs={{0,7},{1,2},{2,1},{3,4},{4,3},{5,6},{6,5},{7,0},{8,15},{9,10},{10,... | collective-permute-start | bytes 414728 | tf_op jit(solution)/shard_map/ppermute | solution.py:592
  18.1 0.8 %collective-permute-start.3 = (f32[15,3,4,192]{3,2,1,0:T(4,128)S(1)}, f32[15,3,4,192]{3,2,1,0:T(4,128)S(1)}, u32[]{:S(2)}, u32[]{:S(2)}) collective-permute-start(f32[15,3,4,192]{3,2,1,0:T(4,128)S(1)} %get-tuple-element.76), channel_id=1, source_target_pairs={{0,1},{1,0},{2,3},{3,2},{4,5},{5,4},{6,7},{7,6},{8,9},{9,8},{10,11... | collective-permute-start | bytes 414728 | tf_op jit(solution)/shard_map/ppermute | solution.py:593
  18.9 3.8 %core_columns.1 = (bf16[15,15,16,384]{3,2,1,0:T(8,128)(2,1)S(1)}, f32[15,15,16,192]{3,2,1,0:T(8,128)S(1)}, f32[15,3,16,192]{3,2,1,0:T(8,128)S(1)}, f32[15,3,16,1...) custom-call(s32[2,6]{1,0:T(2,128)S(1)} %bitcast.12, ...), custom_call_target="tpu_custom_call", output_to_operand_aliasing={{0}: (2, {}), {1}: (3, {})} | custom-call | tf_op jit(solution)/shard_map/core_columns/pallas_call | solution.py:400
  22.7 2.5 %collective-permute-done.2.far_in = f32[15,3,4,192]{3,2,1,0:T(4,128)S(1)} collective-permute-done((f32[15,3,4,192]{3,2,1,0:T(4,128)S(1)}, f32[15,3,4,192]{3,2,1,0:T(4,128)S(1)}, u32[]{:S(2)}, u32[]{:S(2)}) %collective-permute-start.2) | collective-permute-done | bytes 138272 | tf_op jit(solution)/shard_map/ppermute | solution.py:592
  25.2 0.0 collective-permute-done.3.near_in
  25.2 6.6 %outer_rows.1 = (bf16[15,15,16,384]{3,2,1,0:T(8,128)(2,1)S(1)}, f32[15,15,16,192]{3,2,1,0:T(8,128)S(1)}, f32[3,63,4,128]{3,2,1,0:T(4,128)S(1)}, f32[3,63,4,128]{3,2,1,0:T(4,128)S(1)}, f32[2,6,36,4,192]{4,3,2,1,0:T(4,128)S(1)}) custom-call(s32[2,6]{1,0:T(2,128)S(1)} %bitcast.13, s32[2,6]{1,0:T(2,128)S(1)} %bitcast.16, ...), custom_call_target="tpu_custom_call", output_to_operand_aliasing={{0}: (2, {}), {1}: (3, {})} | custom-call | tf_op jit(solution)/shard_map/outer_rows/pallas_call | solution.py:449
  31.8 0.1 collective-permute-start.4
  31.9 3.0 %collective-permute-start.5 = (f32[3,63,4,128]{3,2,1,0:T(4,128)S(1)}, f32[3,63,4,128]{3,2,1,0:T(4,128)S(1)}, u32[]{:S(2)}, u32[]{:S(2)}) collective-permute-start(f32[3,63,4,128]{3,2,1,0:T(4,128)S(1)} %get-tuple-element.87), channel_id=1, source_target_pairs={{0,248},{8,16},{16,8},{24,32},{32,24},{40,48},{48,40},{56,64},{64,... | collective-permute-start | bytes 1161224 | tf_op jit(solution)/shard_map/ppermute | solution.py:592
  34.8 6.2 %inner_rows.1 = (f32[9,36,4,192]{3,2,1,0:T(4,128)}, f32[9,36,4,192]{3,2,1,0:T(4,128)}, f32[9,9,16,192]{3,2,1,0:T(8,128)S(1)}, f32[9,3,4,192]{3,2,1,0:T(4,128)S(1...) custom-call(s32[2,6]{1,0:T(2,128)S(1)} %bitcast.14, ...), custom_call_target="tpu_custom_call" | custom-call | tf_op jit(solution)/shard_map/inner_rows/pallas_call | solution.py:500
  41.0 1.9 %collective-permute-done.5.far = f32[3,63,4,128]{3,2,1,0:T(4,128)S(1)} collective-permute-done((f32[3,63,4,128]{3,2,1,0:T(4,128)S(1)}, f32[3,63,4,128]{3,2,1,0:T(4,128)S(1)}, u32[]{:S(2)}, u32[]{:S(2)}) %collective-permute-start.5) | collective-permute-done | bytes 387104 | tf_op jit(solution)/shard_map/ppermute | solution.py:592
  42.9 0.3 sums.1
  43.3 2.1 %collective-permute-start.6 = (f32[9,3,4,192]{3,2,1,0:T(4,128)S(1)}, f32[9,3,4,192]{3,2,1,0:T(4,128)S(1)}, u32[]{:S(2)}, u32[]{:S(2)}) collective-permute-start(f32[9,3,4,192]{3,2,1,0:T(4,128)S(1)} %get-tuple-element.93), channel_id=1, source_target_pairs={{0,7},{1,2},{2,1},{3,4},{4,3},{5,6},{6,5},{7,0},{8,15},{9,10},{10,... | collective-permute-start | bytes 248840 | tf_op jit(solution)/shard_map/ppermute | solution.py:592
  45.4 2.6 %all_columns.1 = (f32[9,36,4,192]{3,2,1,0:T(4,128)S(1)}, f32[9,3,8,192]{3,2,1,0:T(8,128)S(1)}, f32[9,3,8,192]{3,2,1,0:T(8,128)S(1)}, f32[9,3,8,384]{3,2,1,0:T(8,128)S(1)}) custom-call(f32[2,3,42,4,192]{4,3,2,1,0:T(4,128)S(1)} %get-tuple-element.95.beyond, f32[9,9,16,192]{3,2,1,0:T(8,128)S(1)} %get-tuple-element.96.acc_mid, ...), custom_call_target="tpu_custom_call" | custom-call | tf_op jit(solution)/shard_map/all_columns/pallas_call | solution.py:545
  48.0 2.2 %collective-permute-done.6.far = f32[9,3,4,192]{3,2,1,0:T(4,128)S(1)} collective-permute-done((f32[9,3,4,192]{3,2,1,0:T(4,128)S(1)}, f32[9,3,4,192]{3,2,1,0:T(4,128)S(1)}, u32[]{:S(2)}, u32[]{:S(2)}) %collective-permute-start.6) | collective-permute-done | bytes 82976 | tf_op jit(solution)/shard_map/ppermute | solution.py:592
  50.2 1.6 %edge_columns.1 = f32[9,36,4,192]{3,2,1,0:T(4,128)} custom-call(f32[9,3,4,192]{3,2,1,0:T(4,128)S(1)} %collective-permute-done.6.far, f32[9,3,4,192]{3,2,1,0:T(4,128)S(1)} %collective-permute-done.7.near, f32[9,36,4,192]{3,2,1,0:T(4,128)S(1)} %get-tuple-element.101.states, f32[9,3,8,192]{3,2,1,0:T(8,128)S(1)} %get-tuple-element.102.edge_m, ...), custom_call_target="tpu_custom_call" | custom-call | tf_op jit(solution)/shard_map/edge_columns/pallas_call | solution.py:576
  (5 shorter events, 0.0 us)
Async XLA Ops:
  2.1 15.0 %collective-permute-start = (f32[3,54,4,128]{3,2,1,0:T(4,128)S(1)}, f32[3,54,4,128]{3,2,1,0:T(4,128)S(1)}, u32[]{:S(2)}, u32[]{:S(2)}) collective-permute-start(f32[3,54,4,128]{3,2,1,0:T(4,128)S(1)} %get-tuple-element.58), channel_id=1, source_target_pairs={{0,8},{8,0},{16,24},{24,16},{32,40},{40,32},{48,56},{56,48},{64,72... | collective-permute-start | bytes 995336 | tf_op jit(solution)/shard_map/ppermute | solution.py:593
  2.2 14.9 %collective-permute-start.1 = (f32[3,54,4,128]{3,2,1,0:T(4,128)S(1)}, f32[3,54,4,128]{3,2,1,0:T(4,128)S(1)}, u32[]{:S(2)}, u32[]{:S(2)}) collective-permute-start(f32[3,54,4,128]{3,2,1,0:T(4,128)S(1)} %get-tuple-element.59), channel_id=1, source_target_pairs={{0,248},{8,16},{16,8},{24,32},{32,24},{40,48},{48,40},{56,64},{64,... | collective-permute-start | bytes 995336 | tf_op jit(solution)/shard_map/ppermute | solution.py:592
  17.1 1.8 %copy-start = (s32[6,2]{0,1:T(2,128)S(1)}, s32[6,2]{0,1:T(2,128)}, u32[]{:S(2)}) copy-start(s32[6,2]{0,1:T(2,128)} %param.17) | copy-start | bytes 148
  17.1 1.8 %copy-start.1 = (s32[6,2]{0,1:T(2,128)S(1)}, s32[6,2]{0,1:T(2,128)}, u32[]{:S(2)}) copy-start(s32[6,2]{0,1:T(2,128)} %param.18) | copy-start | bytes 148
  17.4 7.7 %collective-permute-start.2 = (f32[15,3,4,192]{3,2,1,0:T(4,128)S(1)}, f32[15,3,4,192]{3,2,1,0:T(4,128)S(1)}, u32[]{:S(2)}, u32[]{:S(2)}) collective-permute-start(f32[15,3,4,192]{3,2,1,0:T(4,128)S(1)} %get-tuple-element.75), channel_id=1, source_target_pairs={{0,7},{1,2},{2,1},{3,4},{4,3},{5,6},{6,5},{7,0},{8,15},{9,10},{10,... | collective-permute-start | bytes 414728 | tf_op jit(solution)/shard_map/ppermute | solution.py:592
  18.1 7.1 %collective-permute-start.3 = (f32[15,3,4,192]{3,2,1,0:T(4,128)S(1)}, f32[15,3,4,192]{3,2,1,0:T(4,128)S(1)}, u32[]{:S(2)}, u32[]{:S(2)}) collective-permute-start(f32[15,3,4,192]{3,2,1,0:T(4,128)S(1)} %get-tuple-element.76), channel_id=1, source_target_pairs={{0,1},{1,0},{2,3},{3,2},{4,5},{5,4},{6,7},{7,6},{8,9},{9,8},{10,11... | collective-permute-start | bytes 414728 | tf_op jit(solution)/shard_map/ppermute | solution.py:593
  31.8 9.3 %collective-permute-start.4 = (f32[3,63,4,128]{3,2,1,0:T(4,128)S(1)}, f32[3,63,4,128]{3,2,1,0:T(4,128)S(1)}, u32[]{:S(2)}, u32[]{:S(2)}) collective-permute-start(f32[3,63,4,128]{3,2,1,0:T(4,128)S(1)} %get-tuple-element.86), channel_id=1, source_target_pairs={{0,8},{8,0},{16,24},{24,16},{32,40},{40,32},{48,56},{56,48},{64,72... | collective-permute-start | bytes 1161224 | tf_op jit(solution)/shard_map/ppermute | solution.py:593
  31.9 11.1 %collective-permute-start.5 = (f32[3,63,4,128]{3,2,1,0:T(4,128)S(1)}, f32[3,63,4,128]{3,2,1,0:T(4,128)S(1)}, u32[]{:S(2)}, u32[]{:S(2)}) collective-permute-start(f32[3,63,4,128]{3,2,1,0:T(4,128)S(1)} %get-tuple-element.87), channel_id=1, source_target_pairs={{0,248},{8,16},{16,8},{24,32},{32,24},{40,48},{48,40},{56,64},{64,... | collective-permute-start | bytes 1161224 | tf_op jit(solution)/shard_map/ppermute | solution.py:592
  43.3 6.9 %collective-permute-start.6 = (f32[9,3,4,192]{3,2,1,0:T(4,128)S(1)}, f32[9,3,4,192]{3,2,1,0:T(4,128)S(1)}, u32[]{:S(2)}, u32[]{:S(2)}) collective-permute-start(f32[9,3,4,192]{3,2,1,0:T(4,128)S(1)} %get-tuple-element.93), channel_id=1, source_target_pairs={{0,7},{1,2},{2,1},{3,4},{4,3},{5,6},{6,5},{7,0},{8,15},{9,10},{10,... | collective-permute-start | bytes 248840 | tf_op jit(solution)/shard_map/ppermute | solution.py:592
  45.4 4.8 %collective-permute-start.7 = (f32[9,3,4,192]{3,2,1,0:T(4,128)S(1)}, f32[9,3,4,192]{3,2,1,0:T(4,128)S(1)}, u32[]{:S(2)}, u32[]{:S(2)}) collective-permute-start(f32[9,3,4,192]{3,2,1,0:T(4,128)S(1)} %get-tuple-element.94), channel_id=1, source_target_pairs={{0,1},{1,0},{2,3},{3,2},{4,5},{5,4},{6,7},{7,6},{8,9},{9,8},{10,11... | collective-permute-start | bytes 248840 | tf_op jit(solution)/shard_map/ppermute | solution.py:593
